TPU v7x, 32 devices: a whole 2x2x4 slice. The times are simulated.
32 devices in a mesh: grp: 4 (over y, x), pair: 8 (over z, core).
Axes of the slice: x: 2, y: 2, z: 4, core: 2. Of those that a mesh axis runs over, the one named last changes fastest.
Arguments:
- amplitudes: bfloat16 [24, 24, 9216], P('pair'), may hold values from -6 to 6
- integrals: bfloat16 [9216, 9216], P('pair', 'grp'), may hold values from -0.0625 to 0.0625
- live_counts: int32 [2], replicated, may hold values from 48 to 96, as said below
Outputs:
- residual: bfloat16 [24, 24, 9216], P('pair', None, 'grp')
Inputs may be any that keep to these rules, and one draw needn't show every extreme that they name: `live_counts`: orbital slots at or beyond a count are padding; exactly one of the two counts equals 96.
All inputs are finite; a program needn't handle non-finite values.
Results may differ from a plain program's by a relative error of at most 0.001.
Values may be sent and summed in bfloat16 or wider, within the bound.
A program may use at most 128 MiB of HBM per device.

v0:
```python
import jax
import jax.numpy as jnp
from jax import lax
from jax.sharding import PartitionSpec as P

VB = 96


def on_device(amplitudes, integrals, live_counts):
    occ_rows, occupied, virt_pairs = amplitudes.shape
    slab_cols = integrals.shape[1]
    tile_size = VB
    slab_lanes = slab_cols // tile_size
    position = jnp.arange(virt_pairs)
    keep_pairs = (
        (position // tile_size < live_counts[1]) & (position % tile_size < live_counts[1])
    ).astype(jnp.bfloat16)
    masked = amplitudes * keep_pairs
    flat_rows = masked.reshape(occ_rows * occupied, virt_pairs)
    ladder = jnp.dot(
        flat_rows,
        lax.all_gather(integrals, "pair", axis=0, tiled=True),
        preferred_element_type=jnp.float32,
    )
    blocks = ladder.reshape(occ_rows, occupied, slab_lanes, tile_size)
    mirrored = lax.all_to_all(
        lax.all_to_all(blocks, "grp", split_axis=3, concat_axis=2, tiled=True),
        "pair",
        split_axis=1,
        concat_axis=0,
        tiled=True,
    )
    summed = blocks + jnp.transpose(mirrored, (1, 0, 3, 2))
    first_virt = lax.axis_index("grp") * slab_lanes + jnp.arange(slab_lanes)
    second_virt = jnp.arange(tile_size)
    keep_out = (
        (first_virt[:, None] < live_counts[0]) & (second_virt[None, :] < live_counts[0])
    ).astype(jnp.float32)
    return (summed * keep_out).reshape(occ_rows, occupied, slab_cols).astype(jnp.bfloat16)


def solution(mesh):
    return jax.shard_map(
        on_device,
        mesh=mesh,
        in_specs=(P("pair", None, None), P("pair", "grp"), P()),
        out_specs=P("pair", None, "grp"),
        check_vma=False,
    )
```

profile of v0, /device:TPU:0, one launch (start us, length us, event | category | flops | bytes accessed | tf_op | source)
XLA Modules:
  0.0 521.9 jit_solution(7141288464525714496)
XLA Ops:
  6.5 0.0 copy-start.1
  6.5 0.0 all-gather.2.cloned.1.call-start
  6.5 0.7 all-gather.2.cloned.1.call-update
  7.3 0.0 copy-done.1
  7.3 0.7 fusion.17
  7.9 0.7 fusion.16
  8.7 366.3 %all-gather.2.cloned.1.call-done = bf16[9216,2304]{1,0:T(8,128)(2,1)} async-done(((bf16[1152,2304]{1,0:T(8,128)(2,1)}), bf16[9216,2304]{1,0:T(8,128)(2,1)}) %all-gather.2.cloned.1.call-update) | async-done | bytes 42467344 | tf_op jit(solution)/shard_map/all_gather | solution.py:22
  374.9 0.0 copy-start.2
  374.9 54.8 %copy.10 = bf16[2304,9216]{1,0:T(8,128)(2,1)} copy(bf16[2304,9216]{0,1:T(8,128)(2,1)} %bitcast.30) | data formatting | bytes 84934656 | tf_op jit(solution)/shard_map/dot_general | solution.py:20
  429.7 0.0 copy-done.2
  429.7 21.4 %fusion = f32[3,24,24,96]{3,1,2,0:T(8,128)} fusion(bf16[24,96,9216,1]{2,1,0,3:T(8,128)(2,1)} %bitcast.31, bf16[3,24,9216]{2,1,0:T(8,128)(2,1)S(1)} %copy-done.2, bf16[9216]{0:T(1024)(128)(2,1)S(1)} %fusion.16), kind=kOutput, calls=%fused_computation | convolution fusion | flops 3060301824 | bytes 44476416 | tf_op jit(solution)/shard_map/dot_general | solution.py:20
  451.2 2.9 copy.11
  454.1 3.4 reshape.69
  457.5 14.5 %all_to_all.36 = f32[4,1,41472]{2,1,0:T(1,128)S(1)} all-to-all(f32[4,1,41472]{2,1,0:T(1,128)} %reshape.69), channel_id=1, replica_groups=mesh['grp'=4,'pair'=8] {'grp'}, dimensions={0} | all-to-all | bytes 1327104 | tf_op jit(solution)/shard_map/all_to_all | solution.py:27
  472.0 0.6 broadcast.73
  472.6 3.4 reduce
  475.9 3.8 reshape.70
  479.7 3.1 copy.12
  482.8 3.2 all_to_all.29
  486.1 0.0 copy-start
  486.1 1.0 copy.13
  487.1 3.5 all-to-all-start.1
  490.6 0.7 iota_compare_fusion
  491.3 0.7 add_compare_fusion
  491.9 0.1 and_convert_fusion
  492.0 21.6 %all-to-all-done.1 = f32[3,24,96,24]{2,3,0,1:T(8,128)S(1)} async-done(((f32[3,24,96,24]{2,3,0,1:T(8,128)}), f32[3,24,96,24]{2,3,0,1:T(8,128)S(1)}, u32[]{:S(2)}, u32[]{:S(2)}) %all-to-all-start.1) | async-done | bytes 663584 | tf_op jit(solution)/shard_map/all_to_all | solution.py:26
  513.6 0.1 copy.15
  513.7 0.0 copy-done
  513.7 0.2 fusion.4
  513.9 0.1 copy.17
  514.0 1.1 convert_element_type.23
Async XLA Ops:
  6.5 0.7 copy-start.1
  6.5 368.4 %all-gather.2.cloned.1.call-start = ((), (), s32[]{:S(2)}) async-start(), calls=%async_computation.2 | async-start | bytes 47775744 | tf_op jit(solution)/shard_map/all_gather | solution.py:22
  374.9 54.8 %copy-start.2 = (bf16[3,24,9216]{2,1,0:T(8,128)(2,1)S(1)}, bf16[3,24,9216]{2,1,0:T(8,128)(2,1)}, u32[]{:S(2)}) copy-start(bf16[3,24,9216]{2,1,0:T(8,128)(2,1)} %param.3) | copy-start | bytes 3981316
  486.1 27.6 %copy-start = (f32[3,24,24,96]{3,1,2,0:T(8,128)S(1)}, f32[3,24,24,96]{3,1,2,0:T(8,128)}, u32[]{:S(2)}) copy-start(f32[3,24,24,96]{3,1,2,0:T(8,128)} %fusion) | copy-start | bytes 1990660
  487.1 26.6 %all-to-all-start.1 = ((f32[3,24,96,24]{2,3,0,1:T(8,128)}), f32[3,24,96,24]{2,3,0,1:T(8,128)S(1)}, u32[]{:S(2)}, u32[]{:S(2)}) async-start(f32[3,24,96,24]{2,3,0,1:T(8,128)} %copy.13), calls=%async_computation.1 | async-start | bytes 1769472 | tf_op jit(solution)/shard_map/all_to_all | solution.py:26
Sparse Core Ops, SparseCore 0:
  9.0 365.8 all-gather.1
where the time goes:
time: 524 us; the launch traced here: 522 us
  waiting for transfers between devices  389 us (74%)
  local copies, waits for them, and re-layouts  74.6 us (14%)
  matrix products  21.4 us (4%)
  blocking collectives  14.5 us (3%)
  between operations  13.5 us (3%)
  other arithmetic  5.68 us (1%)
    all_gather x1, waiting for transfers between devices, on_device(): lax.all_gather(integrals, 'pair', axis=0, tiled=True)  366 us
    dot_general x2, local copies, waits for them, and re-layouts, on_device(): jnp.dot(flat_rows, lax.all_gather(integrals, 'pair', axis=0, tiled=True),...  57.7 us
    all_to_all x1, waiting for transfers between devices, on_device(): lax.all_to_all(lax.all_to_all(blocks, 'grp', split_axis=3, concat_axis=2,...  21.6 us
    dot_general x1, matrix products, on_device(): jnp.dot(flat_rows, lax.all_gather(integrals, 'pair', axis=0, tiled=True),...  21.4 us
    all_to_all x1, blocking collectives, on_device(): lax.all_to_all(blocks, 'grp', split_axis=3, concat_axis=2, tiled=True)  14.5 us
  transfers between devices with their start and end apart: 2, of which 2 were waited for; matrix products, arithmetic and copies ran while one was open for 1% of the time, Pallas kernels for 0%

commit v1 on v0

--- a/solution.py
+++ b/solution.py
@@ -8,20 +8,19 @@
 
 def on_device(amplitudes, integrals, live_counts):
     occ_rows, occupied, virt_pairs = amplitudes.shape
-    slab_cols = integrals.shape[1]
+    my_pairs, slab_cols = integrals.shape
     tile_size = VB
     slab_lanes = slab_cols // tile_size
-    position = jnp.arange(virt_pairs)
+    rows = occ_rows * occupied
+    flat_rows = lax.all_to_all(
+        amplitudes.reshape(rows, virt_pairs), "pair", split_axis=1, concat_axis=0, tiled=True
+    )
+    position = lax.axis_index("pair") * my_pairs + jnp.arange(my_pairs)
     keep_pairs = (
         (position // tile_size < live_counts[1]) & (position % tile_size < live_counts[1])
     ).astype(jnp.bfloat16)
-    masked = amplitudes * keep_pairs
-    flat_rows = masked.reshape(occ_rows * occupied, virt_pairs)
-    ladder = jnp.dot(
-        flat_rows,
-        lax.all_gather(integrals, "pair", axis=0, tiled=True),
-        preferred_element_type=jnp.float32,
-    )
+    partial = jnp.dot(flat_rows * keep_pairs, integrals, preferred_element_type=jnp.float32)
+    ladder = lax.psum_scatter(partial, "pair", scatter_dimension=0, tiled=True)
     blocks = ladder.reshape(occ_rows, occupied, slab_lanes, tile_size)
     mirrored = lax.all_to_all(
         lax.all_to_all(blocks, "grp", split_axis=3, concat_axis=2, tiled=True),

time: 524 us -> 189 us (0.36)
  waiting for transfers between devices: 389 us -> 113 us
  local copies, waits for them, and re-layouts: 74.6 us -> 26.2 us
  matrix products: 21.4 us -> 7.87 us
  starting transfers between devices: 3.55 us -> 10.7 us
    all_gather x1 -> x0, waiting for transfers between devices: 366 us -> none  [on_device(): lax.all_gather(integrals, 'pair', axis=0, tiled=True)]
    reduce_scatter x0 -> x1, waiting for transfers between devices: none -> 59.6 us  [on_device(): ladder = lax.psum_scatter(partial, 'pair', scatter_dimension=0, tiled=True)]
    dot_general x2 -> x0, local copies, waits for them, and re-layouts: 57.7 us -> none  [on_device(): jnp.dot(flat_rows, lax.all_gather(integrals, 'pair', axis=0, tiled=True),...]
    all_to_all x0 -> x1, waiting for transfers between devices: none -> 31.4 us  [on_device(): lax.all_to_all(amplitudes.reshape(rows, virt_pairs), 'pair', split_axis=1...]
    dot_general x1, matrix products: 21.4 us -> 7.87 us  [on_device(): jnp.dot(flat_rows * keep_pairs, integrals, preferred_element_type=jnp.flo...]
    all_to_all x0 -> x1, starting transfers between devices: none -> 6.46 us  [on_device(): lax.all_to_all(amplitudes.reshape(rows, virt_pairs), 'pair', split_axis=1...]
    reshape x0 -> x2, local copies, waits for them, and re-layouts: none -> 5.57 us  [on_device(): blocks = ladder.reshape(occ_rows, occupied, slab_lanes, tile_size)]
  transfers between devices with their start and end apart: 2 -> 3, of which waited for: 2 -> 3; matrix products, arithmetic and copies ran while one was open for 1% -> 1% of each run, Pallas kernels for 0% -> 0%
where the time goes in v1:
time: 189 us
  waiting for transfers between devices  113 us (60%)
  local copies, waits for them, and re-layouts  26.2 us (14%)
  between operations  13.5 us (7%)
  blocking collectives  11.9 us (6%)
  starting transfers between devices  10.7 us (6%)
  matrix products  7.87 us (4%)
  other arithmetic  5.76 us (3%)
    reduce_scatter x1, waiting for transfers between devices, on_device(): ladder = lax.psum_scatter(partial, 'pair', scatter_dimension=0, tiled=True)  59.6 us
    all_to_all x1, waiting for transfers between devices, on_device(): lax.all_to_all(amplitudes.reshape(rows, virt_pairs), 'pair', split_axis=1...  31.4 us
    all_to_all x1, waiting for transfers between devices, on_device(): lax.all_to_all(lax.all_to_all(blocks, 'grp', split_axis=3, concat_axis=2,...  21.6 us
    all_to_all x1, blocking collectives, on_device(): lax.all_to_all(blocks, 'grp', split_axis=3, concat_axis=2, tiled=True)  11.9 us
    all_to_all x4, local copies, waits for them, and re-layouts, on_device(): lax.all_to_all(blocks, 'grp', split_axis=3, concat_axis=2, tiled=True)  8.82 us
    unnamed x7, local copies, waits for them, and re-layouts  8.65 us
    dot_general x1, matrix products, on_device(): jnp.dot(flat_rows * keep_pairs, integrals, preferred_element_type=jnp.flo...  7.87 us
    all_to_all x1, starting transfers between devices, on_device(): lax.all_to_all(amplitudes.reshape(rows, virt_pairs), 'pair', split_axis=1...  6.46 us
  transfers between devices with their start and end apart: 3, of which 3 were waited for; matrix products, arithmetic and copies ran while one was open for 1% of the time, Pallas kernels for 0%

profile of v1, /device:TPU:0, one launch (start us, length us, event | category | flops | bytes accessed | tf_op | source)
XLA Modules:
  0.0 188.5 jit_solution(8321910416570391827)
XLA Ops:
  6.5 1.5 copy.27
  8.1 1.2 copy.14
  9.3 0.0 copy-start.1
  9.3 6.5 %all-to-all-start = ((bf16[72,8,1152]{2,0,1:T(8,128)(2,1)}), bf16[72,8,1152]{2,0,1:T(8,128)(2,1)S(1)}, u32[]{:S(2)}, u32[]{:S(2)}) async-start(bf16[72,8,1152]{2,0,1:T(8,128)(2,1)} %copy.14), calls=%async_computation | async-start | bytes 2654208 | tf_op jit(solution)/shard_map/all_to_all | solution.py:15
  15.7 0.0 reduce-scatter.2.cloned.1.call-start
  15.8 0.0 copy-done.1
  15.8 0.6 fusion.11
  16.4 0.6 fusion.10
  16.9 31.4 %all-to-all-done = bf16[72,8,1152]{2,0,1:T(8,128)(2,1)S(1)} async-done(((bf16[72,8,1152]{2,0,1:T(8,128)(2,1)}), bf16[72,8,1152]{2,0,1:T(8,128)(2,1)S(1)}, u32[]{:S(2)}, u32[]{:S(2)}) %all-to-all-start) | async-done | bytes 1327136 | tf_op jit(solution)/shard_map/all_to_all | solution.py:15
  48.3 0.2 bitcast_multiply_fusion
  48.5 7.9 %fusion.12 = f32[576,2304]{1,0:T(8,128)} fusion(bf16[576,1152]{1,0:T(8,128)(2,1)S(1)} %bitcast_multiply_fusion, bf16[1152,2304]{1,0:T(8,128)(2,1)} %param.4), kind=kOutput, calls=%fused_computation.22 | convolution fusion | flops 3057647616 | bytes 11943936 | tf_op jit(solution)/shard_map/dot_general | solution.py:22
  56.4 0.0 reduce-scatter.2.cloned.1.call-update
  56.4 59.6 %reduce-scatter.2.cloned.1.call-done = f32[72,2304]{1,0:T(8,128)} async-done(((f32[576,2304]{1,0:T(8,128)}), f32[72,2304]{1,0:T(8,128)}) %reduce-scatter.2.cloned.1.call-update) | async-done | bytes 663568 | tf_op jit(solution)/shard_map/reduce_scatter | solution.py:23
  116.0 2.6 %reshape.69 = f32[3,24,24,96]{3,2,1,0:T(8,128)} reshape(f32[72,2304]{1,0:T(8,128)} %reduce-scatter.2.cloned.1.call-done) | data formatting | bytes 1327104 | tf_op jit(solution)/shard_map/reshape | solution.py:24
  118.6 2.9 %copy.15 = f32[3,24,24,96]{2,1,0,3:T(8,128)S(1)} copy(f32[3,24,24,96]{3,2,1,0:T(8,128)} %reshape.69) | data formatting | bytes 1327104 | tf_op jit(solution)/shard_map/reshape | solution.py:24
  121.6 3.4 %reshape.71 = f32[4,1,41472]{2,1,0:T(1,128)} reshape(f32[96,3,24,24]{3,2,1,0:T(8,128)S(1)} %bitcast.37) | data formatting | bytes 1327104
  124.9 11.9 %all_to_all.55 = f32[4,1,41472]{2,1,0:T(1,128)S(1)} all-to-all(f32[4,1,41472]{2,1,0:T(1,128)} %reshape.71), channel_id=1, replica_groups=mesh['grp'=4,'pair'=8] {'grp'}, dimensions={0} | all-to-all | bytes 1327104 | tf_op jit(solution)/shard_map/all_to_all | solution.py:26
  136.9 0.6 broadcast.77
  137.5 3.4 %reduce = f32[4,41472]{1,0:T(4,128)} reduce(f32[4,1,41472]{2,1,0:T(1,128)S(1)} %all_to_all.55, f32[]{:T(128)} %broadcast.77), dimensions={1}, to_apply=%all_to_all.44.reduce_sub_computation | reduce | bytes 1327108 | tf_op jit(solution)/shard_map/all_to_all | solution.py:26
  140.9 3.8 %reshape.72 = f32[96,3,24,24]{3,2,1,0:T(8,128)S(1)} reshape(f32[4,41472]{1,0:T(4,128)} %reduce) | data formatting | bytes 1327104
  144.7 4.0 %copy.30 = f32[3,24,24,4,24]{2,3,4,1,0:T(4,128)} copy(f32[3,24,24,4,24]{2,1,0,4,3:T(8,128)S(1)} %bitcast.35) | data formatting | bytes 1327104 | tf_op jit(solution)/shard_map/all_to_all | solution.py:26
  148.7 3.2 %all_to_all.47 = f32[3,24,96,24]{2,3,1,0:T(8,128)S(1)} reshape(f32[3,24,4,24,24]{3,2,4,1,0:T(4,128)} %bitcast.36) | data formatting | bytes 1327104 | tf_op jit(solution)/shard_map/all_to_all | solution.py:26
  151.9 1.0 copy.18
  152.9 4.2 %all-to-all-start.2 = ((f32[3,24,96,24]{2,3,0,1:T(8,128)}), f32[3,24,96,24]{2,3,0,1:T(8,128)S(1)}, u32[]{:S(2)}, u32[]{:S(2)}) async-start(f32[3,24,96,24]{2,3,0,1:T(8,128)} %copy.18), calls=%async_computation.3 | async-start | bytes 1769472 | tf_op jit(solution)/shard_map/all_to_all | solution.py:25
  157.1 0.0 copy-start
  157.1 0.7 iota_compare_fusion
  157.8 0.7 add_compare_fusion
  158.5 0.1 and_convert_fusion
  158.6 21.6 %all-to-all-done.2 = f32[3,24,96,24]{2,3,0,1:T(8,128)S(1)} async-done(((f32[3,24,96,24]{2,3,0,1:T(8,128)}), f32[3,24,96,24]{2,3,0,1:T(8,128)S(1)}, u32[]{:S(2)}, u32[]{:S(2)}) %all-to-all-start.2) | async-done | bytes 663584 | tf_op jit(solution)/shard_map/all_to_all | solution.py:25
  180.2 0.1 copy.20
  180.2 0.0 copy-done
  180.2 0.1 fusion.1
  180.4 0.6 reshape.70
  180.9 0.8 copy.26
Async XLA Ops:
  9.3 6.5 %copy-start.1 = (s32[2]{0:T(128)S(1)}, s32[2]{0:T(128)}, u32[]{:S(2)}) copy-start(s32[2]{0:T(128)} %param.5) | copy-start | bytes 28
  9.3 39.0 %all-to-all-start = ((bf16[72,8,1152]{2,0,1:T(8,128)(2,1)}), bf16[72,8,1152]{2,0,1:T(8,128)(2,1)S(1)}, u32[]{:S(2)}, u32[]{:S(2)}) async-start(bf16[72,8,1152]{2,0,1:T(8,128)(2,1)} %copy.14), calls=%async_computation | async-start | bytes 2654208 | tf_op jit(solution)/shard_map/all_to_all | solution.py:15
  15.7 100.3 %reduce-scatter.2.cloned.1.call-start = ((), (), s32[]{:S(2)}) async-start(), calls=%async_computation.4 | async-start | bytes 5971968 | tf_op jit(solution)/shard_map/reduce_scatter | solution.py:23
  152.9 27.3 %all-to-all-start.2 = ((f32[3,24,96,24]{2,3,0,1:T(8,128)}), f32[3,24,96,24]{2,3,0,1:T(8,128)S(1)}, u32[]{:S(2)}, u32[]{:S(2)}) async-start(f32[3,24,96,24]{2,3,0,1:T(8,128)} %copy.18), calls=%async_computation.3 | async-start | bytes 1769472 | tf_op jit(solution)/shard_map/all_to_all | solution.py:25
  157.1 23.1 %copy-start = (f32[3,24,24,96]{3,2,1,0:T(8,128)S(1)}, f32[3,24,24,96]{3,2,1,0:T(8,128)}, u32[]{:S(2)}) copy-start(f32[3,24,24,96]{3,2,1,0:T(8,128)} %reshape.69) | copy-start | bytes 1990660
Sparse Core Ops, SparseCore 0:
  56.5 59.4 reduce-scatter.1

commit v2 on v1

--- a/solution.py
+++ b/solution.py
@@ -1,12 +1,348 @@
+import functools
+
 import jax
 import jax.numpy as jnp
 from jax import lax
+from jax.experimental import pallas as pl
+from jax.experimental.pallas import tpu as pltpu
 from jax.sharding import PartitionSpec as P
 
 VB = 96
-
-
-def on_device(amplitudes, integrals, live_counts):
+STEPS = 32767.0
+MESH = pl.DeviceIdType.MESH
+VMEM_BYTES = 50 * 2**20
+
+
+def quantize(value):
+    peak = jnp.maximum(jnp.max(jnp.abs(value), axis=0, keepdims=True), 1e-33)
+    whole = jnp.floor(value * (STEPS / peak) + 0.5).astype(jnp.int32)
+    half = value.shape[1] // 2
+    stacked = jnp.concatenate([whole[:, :half], whole[:, half:]], axis=0)
+    return stacked.astype(jnp.int16), peak
+
+
+def dequantize(stacked, peak):
+    rows = stacked.shape[0] // 2
+    wide = stacked.astype(jnp.int32).astype(jnp.float32)
+    return jnp.concatenate([wide[:rows], wide[rows:]], axis=1) * (peak * (1.0 / STEPS))
+
+
+def kernel(
+    sizes, live_ref, amp_ref, w_hbm, out_ref,
+    w_ref, t_ref, tt_ref, mask_ref, part_ref, cross_ref, send_q, send_s,
+    recv_q, recv_s, total_ref, split_ref, turned_ref, mirror_ref,
+    w_sem, t_send, t_fwd, t_recv, x_send, x_recv, q_send, s_send, q_recv, s_recv, m_send, m_recv,
+):
+    grps, pairs, occ_rows, occupied, depth, cols, vb = sizes
+    chips = pairs // 2
+    rows = occ_rows * occupied
+    lanes = cols // vb
+    devices = grps * pairs
+    g, p = lax.axis_index("grp"), lax.axis_index("pair")
+    z, core = p // 2, p % 2
+    sibling = 2 * z + 1 - core
+    me = g * pairs + p
+
+    barrier = pltpu.get_barrier_semaphore()
+
+    @pl.loop(1, devices)
+    def _(step):
+        other = lax.rem(me + step, devices)
+        pl.semaphore_signal(
+            barrier, inc=1, device_id=(other // pairs, lax.rem(other, pairs)), device_id_type=MESH
+        )
+
+    w_copy = pltpu.make_async_copy(w_hbm, w_ref, w_sem)
+    w_copy.start()
+    for c in range(depth // vb):
+        alive = jnp.where(p * (depth // vb) + c < live_ref[1], live_ref[1], 0)
+        lane = lax.broadcasted_iota(jnp.int32, (8, vb), 1)
+        mask_ref[:, c * vb:(c + 1) * vb] = jnp.where(lane < alive, 1.0, 0.0)
+    pl.semaphore_wait(barrier, devices - 1)
+
+    def amp_cols(pair):
+        return amp_ref.at[:, pl.ds(pl.multiple_of(pair * depth, 128), depth)]
+
+    def t_copy(src, slot, send_sem, to_grp, to_pair):
+        return pltpu.make_async_remote_copy(
+            src_ref=src, dst_ref=t_ref.at[slot], send_sem=send_sem, recv_sem=t_recv.at[slot],
+            device_id=(to_grp, to_pair), device_id_type=MESH,
+        )
+
+    near_low = z < chips // 2
+
+    def group_of(step):
+        low = jnp.where(step < chips - 1 - z, chips - 1 - step, step - (chips - 1 - z))
+        high = jnp.where(step < z, step, chips - 1 - (step - z))
+        return jnp.where(step == chips - 1, z, jnp.where(near_low, low, high))
+
+    grp_src, grp_dst = lax.rem(g, 2), g // 2
+    sends_t = core == grp_src
+    relays_t = core == grp_dst
+
+    def z_copy(step):
+        to = 2 * group_of(step) + grp_dst
+        return t_copy(amp_cols(to), p, t_send.at[step], g, to)
+
+    own_copy = pltpu.make_async_copy(amp_cols(p), t_ref.at[p], t_recv.at[p])
+    sib_copy = t_copy(amp_cols(sibling), p, t_send.at[chips - 1], g, sibling)
+
+    @pl.when(sends_t)
+    def _():
+        @pl.loop(0, chips - 1)
+        def _(step):
+            z_copy(step).start()
+
+    own_copy.start()
+    sib_copy.start()
+
+    def relay_copy(step, hop):
+        slot = 2 * group_of(step) + grp_src
+        return t_copy(t_ref.at[slot], slot, t_fwd.at[step, hop - 1], lax.rem(g + hop, grps), p)
+
+    def relay(step):
+        @pl.when(relays_t)
+        def _():
+            slot = 2 * group_of(step) + grp_src
+            t_copy(t_ref.at[slot], slot, t_send.at[0], g, p).wait_recv()
+
+            @pl.loop(1, grps)
+            def _(hop):
+                relay_copy(step, hop).start()
+
+    def cross_copy(group):
+        return pltpu.make_async_remote_copy(
+            src_ref=part_ref.at[group, pl.ds(pl.multiple_of((1 - core) * rows, 8), rows)],
+            dst_ref=cross_ref.at[group], send_sem=x_send.at[group], recv_sem=x_recv.at[group],
+            device_id=(g, sibling), device_id_type=MESH,
+        )
+
+    def chain_copies(step, group, side):
+        to = 2 * (z + 1 - 2 * side) + core
+        quanta = pltpu.make_async_remote_copy(
+            src_ref=send_q.at[step], dst_ref=recv_q.at[side, group],
+            send_sem=q_send.at[step], recv_sem=q_recv.at[side, group],
+            device_id=(g, to), device_id_type=MESH,
+        )
+        scales = pltpu.make_async_remote_copy(
+            src_ref=send_s.at[step], dst_ref=recv_s.at[side, group],
+            send_sem=s_send.at[step], recv_sem=s_recv.at[side, group],
+            device_id=(g, to), device_id_type=MESH,
+        )
+        return quanta, scales
+
+    def arrived(group, side):
+        for copy in chain_copies(0, group, side):
+            copy.wait_recv()
+        total_ref[:, :cols] += dequantize(recv_q[side, group], recv_s[side, group])
+
+    def own_sum(group):
+        cross_copy(group).wait_recv()
+        mine = part_ref[group, pl.ds(pl.multiple_of(core * rows, 8), rows), :]
+        total_ref[:, :cols] = mine + cross_ref[group]
+
+    relay(0)
+    w_copy.wait()
+    total_ref[:, cols:] = jnp.zeros((rows, total_ref.shape[1] - cols), jnp.float32)
+
+    @pl.loop(0, chips)
+    def _(step):
+        group = group_of(step)
+
+        @pl.when(step < chips - 2)
+        def _():
+            relay(step + 1)
+
+        for c in range(2):
+            slot = 2 * group + c
+            local = step == chips - 1
+            relayed = jnp.logical_and(relays_t, c == grp_src)
+
+            @pl.when(jnp.logical_and(local, c == core))
+            def _():
+                own_copy.wait()
+
+            @pl.when(jnp.logical_or(
+                jnp.logical_and(local, c != core),
+                jnp.logical_and(jnp.logical_not(local), jnp.logical_not(relayed)),
+            ))
+            def _():
+                t_copy(t_ref.at[slot], slot, t_send.at[0], g, p).wait_recv()
+
+        both = jnp.concatenate(
+            [t_ref[2 * group].astype(jnp.float32), t_ref[2 * group + 1].astype(jnp.float32)], axis=0
+        )
+        tt_ref[...] = (both * mask_ref[:1, :]).astype(jnp.bfloat16)
+
+        @pl.loop(0, cols // 256)
+        def _(tile):
+            at = pl.ds(pl.multiple_of(tile * 256, 256), 256)
+            part_ref[group, :, at] = jnp.dot(
+                tt_ref[...], w_ref[:, at], preferred_element_type=jnp.float32
+            )
+
+        cross_copy(group).start()
+
+        @pl.when(step < chips - 1)
+        def _():
+            own_sum(group)
+            side = jnp.where(group > z, 0, 1)
+            first = jnp.where(side == 0, z == 0, z == chips - 1)
+
+            @pl.when(jnp.logical_not(first))
+            def _():
+                arrived(group, side)
+
+            quanta, peak = quantize(total_ref[:, :cols])
+            send_q[step] = quanta
+            send_s[step] = peak
+            for copy in chain_copies(step, group, side):
+                copy.start()
+
+    own_sum(z)
+
+    @pl.when(z > 0)
+    def _():
+        arrived(z, 0)
+
+    @pl.when(z < chips - 1)
+    def _():
+        arrived(z, 1)
+
+    for a in range(lanes):
+        split_ref[pl.ds(a, rows, stride=lanes), :] = total_ref[:, a * vb:a * vb + 128]
+    per_occ = occupied * lanes
+    per_pair = occ_rows * lanes
+    for i in range(occ_rows):
+        turned = split_ref[i * per_occ:(i + 1) * per_occ, :].T
+        for q in range(pairs):
+            turned_ref[q, :, i * per_pair:(i + 1) * per_pair] = (
+                turned[:vb, q * per_pair:(q + 1) * per_pair]
+            )
+
+    def mirror_copy(step):
+        other = lax.rem(me + step, devices)
+        to_grp, to_pair = other // pairs, lax.rem(other, pairs)
+        return pltpu.make_async_remote_copy(
+            src_ref=turned_ref.at[to_pair, pl.ds(pl.multiple_of(to_grp * lanes, 8), lanes)],
+            dst_ref=mirror_ref.at[me], send_sem=m_send.at[step], recv_sem=m_recv.at[me],
+            device_id=(to_grp, to_pair), device_id_type=MESH,
+        )
+
+    @pl.loop(1, devices)
+    def _(step):
+        mirror_copy(step).start()
+
+    mirror_ref[me] = turned_ref[p, pl.ds(pl.multiple_of(g * lanes, 8), lanes), :]
+
+    @pl.loop(1, devices)
+    def _(step):
+        other = lax.rem(me + step, devices)
+        pltpu.make_async_remote_copy(
+            src_ref=mirror_ref.at[other], dst_ref=mirror_ref.at[other], send_sem=m_send.at[step],
+            recv_sem=m_recv.at[other], device_id=(g, sibling), device_id_type=MESH,
+        ).wait_recv()
+
+    @pl.loop(0, pairs)
+    def _(q):
+        for i in range(occ_rows):
+            for j in range(occ_rows):
+                at = pl.ds(pl.multiple_of((j * occupied + q * occ_rows + i) * lanes, 8), lanes)
+                off = (i * occ_rows + j) * lanes
+                for h in range(grps):
+                    split_ref[at, h * lanes:(h + 1) * lanes] += (
+                        mirror_ref[h * pairs + q, :, off:off + lanes]
+                    )
+
+    lane = lax.broadcasted_iota(jnp.int32, (rows, vb), 1)
+    for a in range(lanes):
+        alive = jnp.where(g * lanes + a < live_ref[0], live_ref[0], 0)
+        total_ref[:, a * vb:(a + 1) * vb] = jnp.where(
+            lane < alive, split_ref[pl.ds(a, rows, stride=lanes), :][:, :vb], 0.0
+        )
+    out_ref[...] = total_ref[:, :cols].astype(jnp.bfloat16)
+
+    sib_copy.wait_send()
+
+    @pl.when(sends_t)
+    def _():
+        @pl.loop(0, chips - 1)
+        def _(step):
+            z_copy(step).wait_send()
+
+    @pl.when(relays_t)
+    def _():
+        @pl.loop(0, chips - 1)
+        def _(step):
+            @pl.loop(1, grps)
+            def _(hop):
+                relay_copy(step, hop).wait_send()
+
+    @pl.loop(0, chips)
+    def _(group):
+        cross_copy(group).wait_send()
+
+    @pl.loop(0, chips - 1)
+    def _(step):
+        group = group_of(step)
+        for copy in chain_copies(step, group, jnp.where(group > z, 0, 1)):
+            copy.wait_send()
+
+    @pl.loop(1, devices)
+    def _(step):
+        mirror_copy(step).wait_send()
+
+
+def fused(mesh, amplitudes, integrals, live_counts):
+    occ_rows, occupied, virt_pairs = amplitudes.shape
+    depth, cols = integrals.shape
+    grps, pairs = mesh.shape["grp"], mesh.shape["pair"]
+    rows, chips, devices = occ_rows * occupied, pairs // 2, grps * pairs
+    lanes = cols // VB
+    sizes = (grps, pairs, occ_rows, occupied, depth, cols, VB)
+    block = -(-occ_rows * occ_rows * lanes // 128) * 128
+    f32, bf16, i16 = jnp.float32, jnp.bfloat16, jnp.int16
+    dma = pltpu.SemaphoreType.DMA
+    out = pl.pallas_call(
+        functools.partial(kernel, sizes),
+        out_shape=jax.ShapeDtypeStruct((rows, cols), bf16),
+        in_specs=[
+            pl.BlockSpec(memory_space=pltpu.SMEM),
+            pl.BlockSpec(memory_space=pltpu.VMEM),
+            pl.BlockSpec(memory_space=pl.ANY),
+        ],
+        out_specs=pl.BlockSpec(memory_space=pltpu.VMEM),
+        scratch_shapes=[
+            pltpu.VMEM((depth, cols), bf16),
+            pltpu.VMEM((pairs, rows, depth), bf16),
+            pltpu.VMEM((2 * rows, depth), bf16),
+            pltpu.VMEM((8, depth), f32),
+            pltpu.VMEM((chips, 2 * rows, cols), f32),
+            pltpu.VMEM((chips, rows, cols), f32),
+            pltpu.VMEM((chips - 1, 2 * rows, cols // 2), i16),
+            pltpu.VMEM((chips - 1, 1, cols), f32),
+            pltpu.VMEM((2, chips, 2 * rows, cols // 2), i16),
+            pltpu.VMEM((2, chips, 1, cols), f32),
+            pltpu.VMEM((rows, cols + 128), f32),
+            pltpu.VMEM((rows * lanes, 128), f32),
+            pltpu.VMEM((pairs, VB, block), f32),
+            pltpu.VMEM((devices, lanes, block), f32),
+            dma(()), dma((chips,)), dma((chips - 1, grps - 1)), dma((pairs,)),
+            dma((chips,)), dma((chips,)), dma((chips - 1,)), dma((chips - 1,)),
+            dma((2, chips)), dma((2, chips)), dma((devices,)), dma((devices,)),
+        ],
+        compiler_params=pltpu.CompilerParams(
+            collective_id=0, has_side_effects=True, vmem_limit_bytes=VMEM_BYTES
+        ),
+        cost_estimate=pl.CostEstimate(
+            flops=4 * pairs // 2 * rows * depth * cols,
+            bytes_accessed=2 * depth * cols, transcendentals=0,
+        ),
+    )(live_counts, amplitudes.reshape(rows, virt_pairs), integrals)
+    return out.reshape(occ_rows, occupied, cols)
+
+
+def gathered(mesh, amplitudes, integrals, live_counts):
     occ_rows, occupied, virt_pairs = amplitudes.shape
     my_pairs, slab_cols = integrals.shape
     tile_size = VB
@@ -38,9 +374,18 @@
     return (summed * keep_out).reshape(occ_rows, occupied, slab_cols).astype(jnp.bfloat16)
 
 
+def on_device(mesh, amplitudes, integrals, live_counts):
+    occ_rows, occupied, virt_pairs = amplitudes.shape
+    depth, cols = integrals.shape
+    rows, pairs = occ_rows * occupied, mesh.shape["pair"]
+    held = 2 * depth * cols + rows * cols * (8 * pairs + 8) + 6 * rows * virt_pairs
+    fits = held < VMEM_BYTES and mesh.shape["grp"] == 4
+    return (fused if fits else gathered)(mesh, amplitudes, integrals, live_counts)
+
+
 def solution(mesh):
     return jax.shard_map(
-        on_device,
+        functools.partial(on_device, mesh),
         mesh=mesh,
         in_specs=(P("pair", None, None), P("pair", "grp"), P()),
         out_specs=P("pair", None, "grp"),

time: 189 us -> 74.9 us (0.40)
  waiting for transfers between devices: 113 us -> 0 us
  Pallas kernels: 0 us -> 72 us
  local copies, waits for them, and re-layouts: 26.2 us -> 2.7 us
  between operations: 13.5 us -> 0.01 us
  blocking collectives: 11.9 us -> 0 us
  starting transfers between devices: 10.7 us -> 0 us
  matrix products: 7.87 us -> 0 us
  other arithmetic: 5.76 us -> 0 us
    pallas_call x0 -> x1, Pallas kernels: none -> 72 us  [fused(): pl.pallas_call(functools.partial(kernel, sizes), out_shape=jax.ShapeDtype...]
    reduce_scatter x1 -> x0, waiting for transfers between devices: 59.6 us -> none  [on_device(): ladder = lax.psum_scatter(partial, 'pair', scatter_dimension=0, tiled=True)]
    all_to_all x2 -> x0, waiting for transfers between devices: 53 us -> none  [the longest x1 31.4 us: on_device(): lax.all_to_all(amplitudes.reshape(rows, virt_pairs), 'pair', split_axis=1...]
    all_to_all x1 -> x0, blocking collectives: 11.9 us -> none  [on_device(): lax.all_to_all(blocks, 'grp', split_axis=3, concat_axis=2, tiled=True)]
    all_to_all x2 -> x0, starting transfers between devices: 10.6 us -> none  [the longest x1 6.46 us: on_device(): lax.all_to_all(amplitudes.reshape(rows, virt_pairs), 'pair', split_axis=1...]
    all_to_all x6 -> x0, local copies, waits for them, and re-layouts: 10.1 us -> none  [the longest x4 8.82 us: on_device(): lax.all_to_all(blocks, 'grp', split_axis=3, concat_axis=2, tiled=True)]
    dot_general x1 -> x0, matrix products: 7.87 us -> none  [on_device(): jnp.dot(flat_rows * keep_pairs, integrals, preferred_element_type=jnp.flo...]
    unnamed x7 -> x5, local copies, waits for them, and re-layouts: 8.65 us -> 2.7 us
  transfers between devices with their start and end apart: 3 -> 0, of which waited for: 3 -> 0; matrix products, arithmetic and copies ran while one was open for 1% -> 0% of each run, Pallas kernels for 0% -> 0%
where the time goes in v2:
time: 74.9 us; the launch traced here: 74.7 us
  Pallas kernels  72 us (96%)
  local copies, waits for them, and re-layouts  2.7 us (4%)
    pallas_call x1, Pallas kernels, fused(): pl.pallas_call(functools.partial(kernel, sizes), out_shape=jax.ShapeDtype...  72 us
    unnamed x5, local copies, waits for them, and re-layouts  2.7 us

profile of v2, /device:TPU:0, one launch (start us, length us, event | category | flops | bytes accessed | tf_op | source)
XLA Modules:
  0.0 74.7 jit_solution(8670600693722896184)
XLA Ops:
  0.0 0.0 copy-start
  0.0 1.3 %copy-done = bf16[3,24,9216]{2,1,0:T(8,128)(2,1)S(1)} copy-done((bf16[3,24,9216]{2,1,0:T(8,128)(2,1)S(1)}, bf16[3,24,9216]{2,1,0:T(8,128)(2,1)}, u32[]{:S(2)}) %copy-start) | copy-done | bytes 1327128
  1.3 0.0 copy-start.1
  1.3 0.7 copy-done.1
  2.0 72.0 %shard_map.37 = bf16[72,2304]{1,0:T(8,128)(2,1)S(1)} custom-call(s32[2]{0:T(128)S(1)} %copy-done.1, bf16[72,9216]{1,0:T(8,128)(2,1)S(1)} %bitcast.3, bf16[1152,2304]{1,0:T(8,128)(2,1)} %w_hbm.1), custom_call_target="tpu_custom_call" | custom-call | flops 3057647616 | bytes 5308416 | tf_op jit(solution)/shard_map/pallas_call | solution.py:306
  74.0 0.7 copy.5
Async XLA Ops:
  0.0 1.3 %copy-start = (bf16[3,24,9216]{2,1,0:T(8,128)(2,1)S(1)}, bf16[3,24,9216]{2,1,0:T(8,128)(2,1)}, u32[]{:S(2)}) copy-start(bf16[3,24,9216]{2,1,0:T(8,128)(2,1)} %param.3) | copy-start | bytes 3981316
  1.3 0.7 copy-start.1

commit v3 on v2

--- a/solution.py
+++ b/solution.py
@@ -1,4 +1,5 @@
 import functools
+import math
 
 import jax
 import jax.numpy as jnp
@@ -10,33 +11,30 @@
 VB = 96
 STEPS = 32767.0
 MESH = pl.DeviceIdType.MESH
-VMEM_BYTES = 50 * 2**20
+VMEM_BYTES = 58 * 2**20
 
 
 def quantize(value):
     peak = jnp.maximum(jnp.max(jnp.abs(value), axis=0, keepdims=True), 1e-33)
     whole = jnp.floor(value * (STEPS / peak) + 0.5).astype(jnp.int32)
-    half = value.shape[1] // 2
-    stacked = jnp.concatenate([whole[:, :half], whole[:, half:]], axis=0)
-    return stacked.astype(jnp.int16), peak
-
-
-def dequantize(stacked, peak):
-    rows = stacked.shape[0] // 2
-    wide = stacked.astype(jnp.int32).astype(jnp.float32)
-    return jnp.concatenate([wide[:rows], wide[rows:]], axis=1) * (peak * (1.0 / STEPS))
+    return whole.astype(jnp.int16), peak
+
+
+def dequantize(quanta, peak):
+    return quanta.astype(jnp.int32).astype(jnp.float32) * (peak * (1.0 / STEPS))
 
 
 def kernel(
     sizes, live_ref, amp_ref, w_hbm, out_ref,
     w_ref, t_ref, tt_ref, mask_ref, part_ref, cross_ref, send_q, send_s,
-    recv_q, recv_s, total_ref, split_ref, turned_ref, mirror_ref,
+    recv_q, recv_s, total_ref, split_ref, half_ref, turned_ref, mirrored_ref, mirror_ref,
     w_sem, t_send, t_fwd, t_recv, x_send, x_recv, q_send, s_send, q_recv, s_recv, m_send, m_recv,
 ):
     grps, pairs, occ_rows, occupied, depth, cols, vb = sizes
     chips = pairs // 2
     rows = occ_rows * occupied
     lanes = cols // vb
+    half_cols, half_lanes = cols // 2, lanes // 2
     devices = grps * pairs
     g, p = lax.axis_index("grp"), lax.axis_index("pair")
     z, core = p // 2, p % 2
@@ -117,33 +115,133 @@
             device_id=(g, sibling), device_id_type=MESH,
         )
 
-    def chain_copies(step, group, side):
+    def chain_copies(half, step, group, side):
         to = 2 * (z + 1 - 2 * side) + core
         quanta = pltpu.make_async_remote_copy(
-            src_ref=send_q.at[step], dst_ref=recv_q.at[side, group],
-            send_sem=q_send.at[step], recv_sem=q_recv.at[side, group],
+            src_ref=send_q.at[half, step], dst_ref=recv_q.at[half, side, group],
+            send_sem=q_send.at[half, step], recv_sem=q_recv.at[half, side, group],
             device_id=(g, to), device_id_type=MESH,
         )
         scales = pltpu.make_async_remote_copy(
-            src_ref=send_s.at[step], dst_ref=recv_s.at[side, group],
-            send_sem=s_send.at[step], recv_sem=s_recv.at[side, group],
+            src_ref=send_s.at[half, step], dst_ref=recv_s.at[half, side, group],
+            send_sem=s_send.at[half, step], recv_sem=s_recv.at[half, side, group],
             device_id=(g, to), device_id_type=MESH,
         )
         return quanta, scales
 
-    def arrived(group, side):
-        for copy in chain_copies(0, group, side):
+    def arrived(half, group, side):
+        for copy in chain_copies(half, 0, group, side):
             copy.wait_recv()
-        total_ref[:, :cols] += dequantize(recv_q[side, group], recv_s[side, group])
-
-    def own_sum(group):
-        cross_copy(group).wait_recv()
-        mine = part_ref[group, pl.ds(pl.multiple_of(core * rows, 8), rows), :]
-        total_ref[:, :cols] = mine + cross_ref[group]
+        total_ref[:, :half_cols] += dequantize(recv_q[half, side, group], recv_s[half, side, group])
+
+    def own_sum(half, group):
+        if half == 0:
+            cross_copy(group).wait_recv()
+        at = slice(half * half_cols, (half + 1) * half_cols)
+        mine = part_ref[group, pl.ds(pl.multiple_of(core * rows, 8), rows), at]
+        total_ref[:, :half_cols] = mine + cross_ref[group, :, at]
+
+    def chain_step(half, step):
+        group = group_of(step)
+        own_sum(half, group)
+        side = jnp.where(group > z, 0, 1)
+        first = jnp.where(side == 0, z == 0, z == chips - 1)
+
+        @pl.when(jnp.logical_not(first))
+        def _():
+            arrived(half, group, side)
+
+        quanta, peak = quantize(total_ref[:, :half_cols])
+        send_q[half, step] = quanta
+        send_s[half, step] = peak
+        for copy in chain_copies(half, step, group, side):
+            copy.start()
+
+    def chain_half(half):
+        @pl.loop(0, chips - 1)
+        def _(step):
+            chain_step(half, step)
+
+    per_occ = occupied * half_lanes
+    per_pair = occ_rows * half_lanes
+    log_step = math.log(2.0) / 256.0
+
+    def mirror_copy(half, step):
+        other = lax.rem(me + step, devices)
+        to_grp, to_pair = other // pairs, lax.rem(other, pairs)
+        return pltpu.make_async_remote_copy(
+            src_ref=mirrored_ref.at[half, to_pair, to_grp], dst_ref=mirror_ref.at[half, me],
+            send_sem=m_send.at[half, step], recv_sem=m_recv.at[half, me],
+            device_id=(to_grp, to_pair), device_id_type=MESH,
+        )
+
+    def finish_half(half):
+        own_sum(half, z)
+
+        @pl.when(z > 0)
+        def _():
+            arrived(half, z, 0)
+
+        @pl.when(z < chips - 1)
+        def _():
+            arrived(half, z, 1)
+
+        for a in range(half_lanes):
+            column = total_ref[:, a * vb:a * vb + 128]
+            split_ref[pl.ds(half * half_lanes + a, rows, stride=lanes), :] = column
+            half_ref[pl.ds(a, rows, stride=half_lanes), :] = column
+        for i in range(occ_rows):
+            turned = half_ref[i * per_occ:(i + 1) * per_occ, :].T
+            for q in range(pairs):
+                turned_ref[q, :, i * per_pair:(i + 1) * per_pair] = (
+                    turned[:vb, q * per_pair:(q + 1) * per_pair]
+                )
+
+        @pl.loop(0, pairs)
+        def _(q):
+            block = turned_ref[q]
+            peak = jnp.maximum(jnp.max(jnp.abs(block), axis=1, keepdims=True), 1e-33)
+            level = jnp.floor(jnp.log(peak) * (1.0 / log_step)) + 2.0
+            whole = jnp.floor(block * (STEPS * jnp.exp(level * -log_step)) + 0.5)
+            lane = lax.broadcasted_iota(jnp.int32, block.shape, 1)
+            whole = jnp.where(lane == 127, level, whole).astype(jnp.int32)
+            for h in range(grps):
+                mirrored_ref[half, q, h] = whole[h * lanes:(h + 1) * lanes].astype(jnp.int16)
+
+        @pl.loop(1, devices)
+        def _(step):
+            mirror_copy(half, step).start()
+
+        mirror_ref[half, me] = mirrored_ref[half, p, g]
+
+    def take_half(half):
+        @pl.loop(1, devices)
+        def _(step):
+            other = lax.rem(me + step, devices)
+            pltpu.make_async_remote_copy(
+                src_ref=mirror_ref.at[half, other], dst_ref=mirror_ref.at[half, other],
+                send_sem=m_send.at[half, step], recv_sem=m_recv.at[half, other],
+                device_id=(g, sibling), device_id_type=MESH,
+            ).wait_recv()
+
+        @pl.loop(0, pairs)
+        def _(q):
+            for h in range(grps):
+                block = mirror_ref[half, h * pairs + q].astype(jnp.int32).astype(jnp.float32)
+                block = block * (jnp.exp(block[:, 127:] * log_step) * (1.0 / STEPS))
+                first = h * lanes + half * half_lanes
+                for i in range(occ_rows):
+                    for j in range(occ_rows):
+                        at = pl.ds(
+                            pl.multiple_of((j * occupied + q * occ_rows + i) * lanes, 8), lanes
+                        )
+                        off = (i * occ_rows + j) * half_lanes
+                        split_ref[at, first:first + half_lanes] += block[:, off:off + half_lanes]
 
     relay(0)
     w_copy.wait()
-    total_ref[:, cols:] = jnp.zeros((rows, total_ref.shape[1] - cols), jnp.float32)
+    total_ref[:, half_cols:] = jnp.zeros((rows, total_ref.shape[1] - half_cols), jnp.float32)
+    turned_ref[...] = jnp.zeros(turned_ref.shape, jnp.float32)
 
     @pl.loop(0, chips)
     def _(step):
@@ -185,82 +283,31 @@
 
         @pl.when(step < chips - 1)
         def _():
-            own_sum(group)
-            side = jnp.where(group > z, 0, 1)
-            first = jnp.where(side == 0, z == 0, z == chips - 1)
-
-            @pl.when(jnp.logical_not(first))
-            def _():
-                arrived(group, side)
-
-            quanta, peak = quantize(total_ref[:, :cols])
-            send_q[step] = quanta
-            send_s[step] = peak
-            for copy in chain_copies(step, group, side):
-                copy.start()
-
-    own_sum(z)
-
-    @pl.when(z > 0)
+            chain_step(0, step)
+
+    at_end = jnp.logical_or(z == 0, z == chips - 1)
+
+    @pl.when(at_end)
     def _():
-        arrived(z, 0)
-
-    @pl.when(z < chips - 1)
+        chain_half(1)
+
+    finish_half(0)
+
+    @pl.when(jnp.logical_not(at_end))
     def _():
-        arrived(z, 1)
-
-    for a in range(lanes):
-        split_ref[pl.ds(a, rows, stride=lanes), :] = total_ref[:, a * vb:a * vb + 128]
-    per_occ = occupied * lanes
-    per_pair = occ_rows * lanes
-    for i in range(occ_rows):
-        turned = split_ref[i * per_occ:(i + 1) * per_occ, :].T
-        for q in range(pairs):
-            turned_ref[q, :, i * per_pair:(i + 1) * per_pair] = (
-                turned[:vb, q * per_pair:(q + 1) * per_pair]
-            )
-
-    def mirror_copy(step):
-        other = lax.rem(me + step, devices)
-        to_grp, to_pair = other // pairs, lax.rem(other, pairs)
-        return pltpu.make_async_remote_copy(
-            src_ref=turned_ref.at[to_pair, pl.ds(pl.multiple_of(to_grp * lanes, 8), lanes)],
-            dst_ref=mirror_ref.at[me], send_sem=m_send.at[step], recv_sem=m_recv.at[me],
-            device_id=(to_grp, to_pair), device_id_type=MESH,
-        )
-
-    @pl.loop(1, devices)
-    def _(step):
-        mirror_copy(step).start()
-
-    mirror_ref[me] = turned_ref[p, pl.ds(pl.multiple_of(g * lanes, 8), lanes), :]
-
-    @pl.loop(1, devices)
-    def _(step):
-        other = lax.rem(me + step, devices)
-        pltpu.make_async_remote_copy(
-            src_ref=mirror_ref.at[other], dst_ref=mirror_ref.at[other], send_sem=m_send.at[step],
-            recv_sem=m_recv.at[other], device_id=(g, sibling), device_id_type=MESH,
-        ).wait_recv()
-
-    @pl.loop(0, pairs)
-    def _(q):
-        for i in range(occ_rows):
-            for j in range(occ_rows):
-                at = pl.ds(pl.multiple_of((j * occupied + q * occ_rows + i) * lanes, 8), lanes)
-                off = (i * occ_rows + j) * lanes
-                for h in range(grps):
-                    split_ref[at, h * lanes:(h + 1) * lanes] += (
-                        mirror_ref[h * pairs + q, :, off:off + lanes]
-                    )
+        chain_half(1)
+
+    finish_half(1)
+    take_half(0)
+    take_half(1)
 
     lane = lax.broadcasted_iota(jnp.int32, (rows, vb), 1)
     for a in range(lanes):
         alive = jnp.where(g * lanes + a < live_ref[0], live_ref[0], 0)
-        total_ref[:, a * vb:(a + 1) * vb] = jnp.where(
+        cross_ref[0, :, a * vb:(a + 1) * vb] = jnp.where(
             lane < alive, split_ref[pl.ds(a, rows, stride=lanes), :][:, :vb], 0.0
         )
-    out_ref[...] = total_ref[:, :cols].astype(jnp.bfloat16)
+    out_ref[...] = cross_ref[0].astype(jnp.bfloat16)
 
     sib_copy.wait_send()
 
@@ -285,12 +332,14 @@
     @pl.loop(0, chips - 1)
     def _(step):
         group = group_of(step)
-        for copy in chain_copies(step, group, jnp.where(group > z, 0, 1)):
-            copy.wait_send()
+        for half in range(2):
+            for copy in chain_copies(half, step, group, jnp.where(group > z, 0, 1)):
+                copy.wait_send()
 
     @pl.loop(1, devices)
     def _(step):
-        mirror_copy(step).wait_send()
+        for half in range(2):
+            mirror_copy(half, step).wait_send()
 
 
 def fused(mesh, amplitudes, integrals, live_counts):
@@ -300,7 +349,6 @@
     rows, chips, devices = occ_rows * occupied, pairs // 2, grps * pairs
     lanes = cols // VB
     sizes = (grps, pairs, occ_rows, occupied, depth, cols, VB)
-    block = -(-occ_rows * occ_rows * lanes // 128) * 128
     f32, bf16, i16 = jnp.float32, jnp.bfloat16, jnp.int16
     dma = pltpu.SemaphoreType.DMA
     out = pl.pallas_call(
@@ -308,7 +356,7 @@
         out_shape=jax.ShapeDtypeStruct((rows, cols), bf16),
         in_specs=[
             pl.BlockSpec(memory_space=pltpu.SMEM),
-            pl.BlockSpec(memory_space=pltpu.VMEM),
+            pl.BlockSpec(memory_space=pl.ANY),
             pl.BlockSpec(memory_space=pl.ANY),
         ],
         out_specs=pl.BlockSpec(memory_space=pltpu.VMEM),
@@ -319,17 +367,19 @@
             pltpu.VMEM((8, depth), f32),
             pltpu.VMEM((chips, 2 * rows, cols), f32),
             pltpu.VMEM((chips, rows, cols), f32),
-            pltpu.VMEM((chips - 1, 2 * rows, cols // 2), i16),
-            pltpu.VMEM((chips - 1, 1, cols), f32),
-            pltpu.VMEM((2, chips, 2 * rows, cols // 2), i16),
-            pltpu.VMEM((2, chips, 1, cols), f32),
-            pltpu.VMEM((rows, cols + 128), f32),
+            pltpu.VMEM((2, chips - 1, rows, cols // 2), i16),
+            pltpu.VMEM((2, chips - 1, 1, cols // 2), f32),
+            pltpu.VMEM((2, 2, chips, rows, cols // 2), i16),
+            pltpu.VMEM((2, 2, chips, 1, cols // 2), f32),
+            pltpu.VMEM((rows, cols // 2 + 128), f32),
             pltpu.VMEM((rows * lanes, 128), f32),
-            pltpu.VMEM((pairs, VB, block), f32),
-            pltpu.VMEM((devices, lanes, block), f32),
+            pltpu.VMEM((rows * lanes // 2, 128), f32),
+            pltpu.VMEM((pairs, VB, 128), f32),
+            pltpu.VMEM((2, pairs, grps, lanes, 128), i16),
+            pltpu.VMEM((2, devices, lanes, 128), i16),
             dma(()), dma((chips,)), dma((chips - 1, grps - 1)), dma((pairs,)),
-            dma((chips,)), dma((chips,)), dma((chips - 1,)), dma((chips - 1,)),
-            dma((2, chips)), dma((2, chips)), dma((devices,)), dma((devices,)),
+            dma((chips,)), dma((chips,)), dma((2, chips - 1)), dma((2, chips - 1)),
+            dma((2, 2, chips)), dma((2, 2, chips)), dma((2, devices)), dma((2, devices)),
         ],
         compiler_params=pltpu.CompilerParams(
             collective_id=0, has_side_effects=True, vmem_limit_bytes=VMEM_BYTES
@@ -379,7 +429,8 @@
     depth, cols = integrals.shape
     rows, pairs = occ_rows * occupied, mesh.shape["pair"]
     held = 2 * depth * cols + rows * cols * (8 * pairs + 8) + 6 * rows * virt_pairs
-    fits = held < VMEM_BYTES and mesh.shape["grp"] == 4
+    block = occ_rows * occ_rows * cols // VB // 2
+    fits = held < VMEM_BYTES and mesh.shape["grp"] == 4 and block < 128
     return (fused if fits else gathered)(mesh, amplitudes, integrals, live_counts)
 
 

time: 74.9 us -> 74.4 us (level)
  local copies, waits for them, and re-layouts: 2.7 us -> 1.72 us
    unnamed x5 -> x1, local copies, waits for them, and re-layouts: 2.7 us -> 1.72 us
where the time goes in v3:
time: 74.4 us; the launch traced here: 74.3 us
  Pallas kernels  72.5 us (97%)
  local copies, waits for them, and re-layouts  1.72 us (2%)
    pallas_call x1, Pallas kernels, fused(): pl.pallas_call(functools.partial(kernel, sizes), out_shape=jax.ShapeDtype...  72.5 us
    unnamed x1, local copies, waits for them, and re-layouts  1.72 us

profile of v3, /device:TPU:0, one launch (start us, length us, event | category | flops | bytes accessed | tf_op | source)
XLA Modules:
  0.0 74.3 jit_solution(16843235616430416392)
XLA Ops:
  0.0 72.5 %shard_map.37 = bf16[72,2304]{1,0:T(8,128)(2,1)} custom-call(s32[2]{0:T(128)} %live_ref.1, bf16[72,9216]{1,0:T(8,128)(2,1)} %bitcast.3, bf16[1152,2304]{1,0:T(8,128)(2,1)} %w_hbm.1), custom_call_target="tpu_custom_call" | custom-call | flops 3057647616 | bytes 5308416 | tf_op jit(solution)/shard_map/pallas_call | solution.py:354
  72.5 1.7 %copy.5 = bf16[3,24,2304]{2,1,0:T(8,128)(2,1)} copy(bf16[3,24,2304]{2,1,0:T(8,128)(2,1)} %bitcast.2) | data formatting | bytes 663552

commit v4 on v3

v4 whole, which is shorter than its diff:
```python
import functools
import math

import jax
import jax.numpy as jnp
from jax import lax
from jax.experimental import pallas as pl
from jax.experimental.pallas import tpu as pltpu
from jax.sharding import PartitionSpec as P

VB = 96
STEPS = 32767.0
MESH = pl.DeviceIdType.MESH
VMEM_BYTES = 58 * 2**20


def quantize(value):
    peak = jnp.maximum(jnp.max(jnp.abs(value), axis=0, keepdims=True), 1e-33)
    whole = jnp.floor(value * (STEPS / peak) + 0.5).astype(jnp.int32)
    return whole.astype(jnp.int16), peak


def dequantize(quanta, peak):
    return quanta.astype(jnp.int32).astype(jnp.float32) * (peak * (1.0 / STEPS))


def kernel(
    sizes, live_ref, amp_ref, w_hbm, out_ref,
    w_ref, t_ref, tt_ref, mask_ref, part_ref, cross_ref, send_q, send_s,
    recv_q, recv_s, total_ref, final_ref, split_ref, piece_ref, mirrored_ref, mirror_ref,
    w_sem, t_send, t_fwd, t_recv, x_send, x_recv, q_send, s_send, q_recv, s_recv, m_send, m_recv,
):
    grps, pairs, occ_rows, occupied, depth, cols, vb = sizes
    chips = pairs // 2
    rows = occ_rows * occupied
    lanes = cols // vb
    chunks, slots = lanes // 8, 127 // lanes
    width = cols // chunks
    devices = grps * pairs
    g, p = lax.axis_index("grp"), lax.axis_index("pair")
    z, core = p // 2, p % 2
    sibling = 2 * z + 1 - core
    me = g * pairs + p

    barrier = pltpu.get_barrier_semaphore()

    @pl.loop(1, devices)
    def _(step):
        other = lax.rem(me + step, devices)
        pl.semaphore_signal(
            barrier, inc=1, device_id=(other // pairs, lax.rem(other, pairs)), device_id_type=MESH
        )

    w_copy = pltpu.make_async_copy(w_hbm, w_ref, w_sem)
    w_copy.start()
    for c in range(depth // vb):
        alive = jnp.where(p * (depth // vb) + c < live_ref[1], live_ref[1], 0)
        lane = lax.broadcasted_iota(jnp.int32, (8, vb), 1)
        mask_ref[:, c * vb:(c + 1) * vb] = jnp.where(lane < alive, 1.0, 0.0)
    pl.semaphore_wait(barrier, devices - 1)

    def amp_cols(pair):
        return amp_ref.at[:, pl.ds(pl.multiple_of(pair * depth, 128), depth)]

    def t_copy(src, slot, send_sem, to_grp, to_pair):
        return pltpu.make_async_remote_copy(
            src_ref=src, dst_ref=t_ref.at[slot], send_sem=send_sem, recv_sem=t_recv.at[slot],
            device_id=(to_grp, to_pair), device_id_type=MESH,
        )

    near_low = z < chips // 2

    def group_of(step):
        low = jnp.where(step < chips - 1 - z, chips - 1 - step, step - (chips - 1 - z))
        high = jnp.where(step < z, step, chips - 1 - (step - z))
        return jnp.where(step == chips - 1, z, jnp.where(near_low, low, high))

    grp_src, grp_dst = lax.rem(g, 2), g // 2
    sends_t = core == grp_src
    relays_t = core == grp_dst

    def z_copy(step):
        to = 2 * group_of(step) + grp_dst
        return t_copy(amp_cols(to), p, t_send.at[step], g, to)

    own_copy = pltpu.make_async_copy(amp_cols(p), t_ref.at[p], t_recv.at[p])
    sib_copy = t_copy(amp_cols(sibling), p, t_send.at[chips - 1], g, sibling)

    @pl.when(sends_t)
    def _():
        @pl.loop(0, chips - 1)
        def _(step):
            z_copy(step).start()

    own_copy.start()
    sib_copy.start()

    def relay_copy(step, hop):
        slot = 2 * group_of(step) + grp_src
        return t_copy(t_ref.at[slot], slot, t_fwd.at[step, hop - 1], lax.rem(g + hop, grps), p)

    def relay(step):
        @pl.when(relays_t)
        def _():
            slot = 2 * group_of(step) + grp_src
            t_copy(t_ref.at[slot], slot, t_send.at[0], g, p).wait_recv()

            @pl.loop(1, grps)
            def _(hop):
                relay_copy(step, hop).start()

    def cross_copy(chunk, group):
        return pltpu.make_async_remote_copy(
            src_ref=part_ref.at[
                chunk, group, pl.ds(pl.multiple_of((1 - core) * rows, 8), rows)
            ],
            dst_ref=cross_ref.at[chunk, group], send_sem=x_send.at[chunk, group],
            recv_sem=x_recv.at[chunk, group], device_id=(g, sibling), device_id_type=MESH,
        )

    def chain_copies(chunk, step, group, side):
        to = 2 * (z + 1 - 2 * side) + core
        quanta = pltpu.make_async_remote_copy(
            src_ref=send_q.at[chunk, step], dst_ref=recv_q.at[chunk, side, group],
            send_sem=q_send.at[chunk, step], recv_sem=q_recv.at[chunk, side, group],
            device_id=(g, to), device_id_type=MESH,
        )
        scales = pltpu.make_async_remote_copy(
            src_ref=send_s.at[chunk, step], dst_ref=recv_s.at[chunk, side, group],
            send_sem=s_send.at[chunk, step], recv_sem=s_recv.at[chunk, side, group],
            device_id=(g, to), device_id_type=MESH,
        )
        return quanta, scales

    def arrived(chunk, group, side, acc):
        for copy in chain_copies(chunk, 0, group, side):
            copy.wait_recv()
        acc[:, :width] += dequantize(recv_q[chunk, side, group], recv_s[chunk, side, group])

    def own_sum(chunk, group, acc):
        cross_copy(chunk, group).wait_recv()
        mine = part_ref[chunk, group, pl.ds(pl.multiple_of(core * rows, 8), rows), :]
        acc[:, :width] = mine + cross_ref[chunk, group]

    def chain_step(chunk, step):
        group = group_of(step)
        own_sum(chunk, group, total_ref)
        side = jnp.where(group > z, 0, 1)
        first = jnp.where(side == 0, z == 0, z == chips - 1)

        @pl.when(jnp.logical_not(first))
        def _():
            arrived(chunk, group, side, total_ref)

        quanta, peak = quantize(total_ref[...])
        send_q[chunk, step] = quanta
        send_s[chunk, step] = peak
        for copy in chain_copies(chunk, step, group, side):
            copy.start()

    def chain_chunk(chunk):
        @pl.loop(0, chips - 1)
        def _(step):
            chain_step(chunk, step)

    log_step = math.log(2.0) / 256.0
    occ_pairs = [(i, j) for i in range(occ_rows) for j in range(occ_rows)]

    def mirror_copy(chunk, step):
        other = lax.rem(me + step, devices)
        to_grp, to_pair = other // pairs, lax.rem(other, pairs)
        return pltpu.make_async_remote_copy(
            src_ref=mirrored_ref.at[chunk, to_pair, to_grp], dst_ref=mirror_ref.at[chunk, me],
            send_sem=m_send.at[chunk, step], recv_sem=m_recv.at[chunk, me],
            device_id=(to_grp, to_pair), device_id_type=MESH,
        )

    def finish_chunk(chunk):
        acc = final_ref.at[chunk]
        own_sum(chunk, z, acc)

        @pl.when(z > 0)
        def _():
            arrived(chunk, z, 0, acc)

        @pl.when(z < chips - 1)
        def _():
            arrived(chunk, z, 1, acc)

        for a in range(8):
            piece_ref[pl.ds(a, rows, stride=8), :] = final_ref[chunk, :, a * vb:a * vb + 128]

        @pl.loop(0, pairs)
        def _(q):
            lane = lax.broadcasted_iota(jnp.int32, (16, 128), 1)
            pieces = [
                piece_ref[
                    pl.ds(pl.multiple_of((i * occupied + q * occ_rows + j) * 8, 8), 8), :
                ]
                for i, j in occ_pairs
            ]
            for h in range(grps):
                ends = []
                for part in (pieces[:slots], pieces[slots:]):
                    packed = jnp.zeros((8, 128), jnp.float32)
                    for at, piece in enumerate(part):
                        shift = ((at - h) * lanes) % 128
                        moved = pltpu.roll(piece, shift, 1) if shift else piece
                        inside = jnp.logical_and(
                            lane[:8] >= at * lanes, lane[:8] < (at + 1) * lanes
                        )
                        packed = jnp.where(inside, moved, packed)
                    ends.append(packed)
                block = jnp.concatenate(ends, axis=0)
                peak = jnp.maximum(jnp.max(jnp.abs(block), axis=1, keepdims=True), 1e-33)
                level = jnp.floor(jnp.log(peak) * (1.0 / log_step)) + 2.0
                whole = jnp.floor(block * (STEPS * jnp.exp(level * -log_step)) + 0.5)
                whole = jnp.where(lane == 127, level, whole).astype(jnp.int32)
                mirrored_ref[chunk, q, h] = whole.astype(jnp.int16)

        @pl.loop(1, devices)
        def _(step):
            mirror_copy(chunk, step).start()

        mirror_ref[chunk, me] = mirrored_ref[chunk, p, g]

    def take_all():
        for chunk in range(chunks):
            @pl.loop(1, devices)
            def _(step):
                other = lax.rem(me + step, devices)
                pltpu.make_async_remote_copy(
                    src_ref=mirror_ref.at[chunk, other], dst_ref=mirror_ref.at[chunk, other],
                    send_sem=m_send.at[chunk, step], recv_sem=m_recv.at[chunk, other],
                    device_id=(g, sibling), device_id_type=MESH,
                ).wait_recv()

        @pl.loop(0, pairs)
        def _(q):
            blocks = []
            for h in range(grps):
                for chunk in range(chunks):
                    block = mirror_ref[chunk, h * pairs + q].astype(jnp.int32).astype(jnp.float32)
                    blocks.append(block * (jnp.exp(block[:, 127:] * log_step) * (1.0 / STEPS)))
            rest = [jnp.zeros((128 - vb, 128), jnp.float32)]
            for end in range(2):
                turned = jnp.concatenate([b[8 * end:8 * end + 8] for b in blocks] + rest, axis=0).T
                for at, (i, j) in enumerate(occ_pairs[end * slots:(end + 1) * slots]):
                    row = (j * occupied + q * occ_rows + i) * lanes
                    split_ref[pl.ds(pl.multiple_of(row, 8), lanes), :] = (
                        turned[at * lanes:(at + 1) * lanes]
                    )

    relay(0)
    w_copy.wait()
    for chunk in range(chunks):
        final_ref[chunk, :, width:] = jnp.zeros((rows, 128), jnp.float32)

    @pl.loop(0, chips)
    def _(step):
        group = group_of(step)

        @pl.when(step < chips - 2)
        def _():
            relay(step + 1)

        for c in range(2):
            slot = 2 * group + c
            local = step == chips - 1
            relayed = jnp.logical_and(relays_t, c == grp_src)

            @pl.when(jnp.logical_and(local, c == core))
            def _():
                own_copy.wait()

            @pl.when(jnp.logical_or(
                jnp.logical_and(local, c != core),
                jnp.logical_and(jnp.logical_not(local), jnp.logical_not(relayed)),
            ))
            def _():
                t_copy(t_ref.at[slot], slot, t_send.at[0], g, p).wait_recv()

        both = jnp.concatenate(
            [t_ref[2 * group].astype(jnp.float32), t_ref[2 * group + 1].astype(jnp.float32)], axis=0
        )
        tt_ref[...] = (both * mask_ref[:1, :]).astype(jnp.bfloat16)

        for chunk in range(chunks):
            @pl.loop(0, width // 256)
            def _(tile):
                at = pl.ds(pl.multiple_of(chunk * width + tile * 256, 256), 256)
                part_ref[chunk, group, :, pl.ds(pl.multiple_of(tile * 256, 256), 256)] = jnp.dot(
                    tt_ref[...], w_ref[:, at], preferred_element_type=jnp.float32
                )

            cross_copy(chunk, group).start()

        @pl.when(step < chips - 1)
        def _():
            chain_step(0, step)

    at_end = jnp.logical_or(z == 0, z == chips - 1)

    @pl.when(at_end)
    def _():
        for chunk in range(1, chunks):
            chain_chunk(chunk)

    for chunk in range(chunks):
        if chunk > 0:
            @pl.when(jnp.logical_not(at_end))
            def _():
                chain_chunk(chunk)
        finish_chunk(chunk)

    take_all()

    lane = lax.broadcasted_iota(jnp.int32, (rows, vb), 1)
    for chunk in range(chunks):
        for a in range(8):
            v = chunk * 8 + a
            alive = jnp.where(g * lanes + v < live_ref[0], live_ref[0], 0)
            both = (
                final_ref[chunk, :, a * vb:(a + 1) * vb]
                + split_ref[pl.ds(v, rows, stride=lanes), :][:, :vb]
            )
            total_ref[:, a * vb:(a + 1) * vb] = jnp.where(lane < alive, both, 0.0)
        out_ref[:, chunk * width:(chunk + 1) * width] = total_ref[...].astype(jnp.bfloat16)

    sib_copy.wait_send()

    @pl.when(sends_t)
    def _():
        @pl.loop(0, chips - 1)
        def _(step):
            z_copy(step).wait_send()

    @pl.when(relays_t)
    def _():
        @pl.loop(0, chips - 1)
        def _(step):
            @pl.loop(1, grps)
            def _(hop):
                relay_copy(step, hop).wait_send()

    @pl.loop(0, chips)
    def _(group):
        for chunk in range(chunks):
            cross_copy(chunk, group).wait_send()

    @pl.loop(0, chips - 1)
    def _(step):
        group = group_of(step)
        for chunk in range(chunks):
            for copy in chain_copies(chunk, step, group, jnp.where(group > z, 0, 1)):
                copy.wait_send()

    @pl.loop(1, devices)
    def _(step):
        for chunk in range(chunks):
            mirror_copy(chunk, step).wait_send()


def fused(mesh, amplitudes, integrals, live_counts):
    occ_rows, occupied, virt_pairs = amplitudes.shape
    depth, cols = integrals.shape
    grps, pairs = mesh.shape["grp"], mesh.shape["pair"]
    rows, chips, devices = occ_rows * occupied, pairs // 2, grps * pairs
    lanes = cols // VB
    chunks = lanes // 8
    width = cols // chunks
    sizes = (grps, pairs, occ_rows, occupied, depth, cols, VB)
    f32, bf16, i16 = jnp.float32, jnp.bfloat16, jnp.int16
    dma = pltpu.SemaphoreType.DMA
    out = pl.pallas_call(
        functools.partial(kernel, sizes),
        out_shape=jax.ShapeDtypeStruct((rows, cols), bf16),
        in_specs=[
            pl.BlockSpec(memory_space=pltpu.SMEM),
            pl.BlockSpec(memory_space=pl.ANY),
            pl.BlockSpec(memory_space=pl.ANY),
        ],
        out_specs=pl.BlockSpec(memory_space=pltpu.VMEM),
        scratch_shapes=[
            pltpu.VMEM((depth, cols), bf16),
            pltpu.VMEM((pairs, rows, depth), bf16),
            pltpu.VMEM((2 * rows, depth), bf16),
            pltpu.VMEM((8, depth), f32),
            pltpu.VMEM((chunks, chips, 2 * rows, width), f32),
            pltpu.VMEM((chunks, chips, rows, width), f32),
            pltpu.VMEM((chunks, chips - 1, rows, width), i16),
            pltpu.VMEM((chunks, chips - 1, 1, width), f32),
            pltpu.VMEM((chunks, 2, chips, rows, width), i16),
            pltpu.VMEM((chunks, 2, chips, 1, width), f32),
            pltpu.VMEM((rows, width), f32),
            pltpu.VMEM((chunks, rows, width + 128), f32),
            pltpu.VMEM((rows * lanes, 128), f32),
            pltpu.VMEM((rows * 8, 128), f32),
            pltpu.VMEM((chunks, pairs, grps, 16, 128), i16),
            pltpu.VMEM((chunks, devices, 16, 128), i16),
            dma(()), dma((chips,)), dma((chips - 1, grps - 1)), dma((pairs,)),
            dma((chunks, chips)), dma((chunks, chips)),
            dma((chunks, chips - 1)), dma((chunks, chips - 1)),
            dma((chunks, 2, chips)), dma((chunks, 2, chips)),
            dma((chunks, devices)), dma((chunks, devices)),
        ],
        compiler_params=pltpu.CompilerParams(
            collective_id=0, has_side_effects=True, vmem_limit_bytes=VMEM_BYTES
        ),
        cost_estimate=pl.CostEstimate(
            flops=4 * pairs // 2 * rows * depth * cols,
            bytes_accessed=2 * depth * cols, transcendentals=0,
        ),
    )(live_counts, amplitudes.reshape(rows, virt_pairs), integrals)
    return out.reshape(occ_rows, occupied, cols)


def gathered(mesh, amplitudes, integrals, live_counts):
    occ_rows, occupied, virt_pairs = amplitudes.shape
    my_pairs, slab_cols = integrals.shape
    tile_size = VB
    slab_lanes = slab_cols // tile_size
    rows = occ_rows * occupied
    flat_rows = lax.all_to_all(
        amplitudes.reshape(rows, virt_pairs), "pair", split_axis=1, concat_axis=0, tiled=True
    )
    position = lax.axis_index("pair") * my_pairs + jnp.arange(my_pairs)
    keep_pairs = (
        (position // tile_size < live_counts[1]) & (position % tile_size < live_counts[1])
    ).astype(jnp.bfloat16)
    partial = jnp.dot(flat_rows * keep_pairs, integrals, preferred_element_type=jnp.float32)
    ladder = lax.psum_scatter(partial, "pair", scatter_dimension=0, tiled=True)
    blocks = ladder.reshape(occ_rows, occupied, slab_lanes, tile_size)
    mirrored = lax.all_to_all(
        lax.all_to_all(blocks, "grp", split_axis=3, concat_axis=2, tiled=True),
        "pair",
        split_axis=1,
        concat_axis=0,
        tiled=True,
    )
    summed = blocks + jnp.transpose(mirrored, (1, 0, 3, 2))
    first_virt = lax.axis_index("grp") * slab_lanes + jnp.arange(slab_lanes)
    second_virt = jnp.arange(tile_size)
    keep_out = (
        (first_virt[:, None] < live_counts[0]) & (second_virt[None, :] < live_counts[0])
    ).astype(jnp.float32)
    return (summed * keep_out).reshape(occ_rows, occupied, slab_cols).astype(jnp.bfloat16)


def on_device(mesh, amplitudes, integrals, live_counts):
    occ_rows, occupied, virt_pairs = amplitudes.shape
    depth, cols = integrals.shape
    rows, pairs = occ_rows * occupied, mesh.shape["pair"]
    held = 2 * depth * cols + rows * cols * (8 * pairs + 8) + 6 * rows * virt_pairs
    lanes = cols // VB
    packs = lanes % 8 == 0 and occ_rows * occ_rows <= 2 * (127 // lanes)
    fits = held < VMEM_BYTES and mesh.shape["grp"] == 4 and packs
    return (fused if fits else gathered)(mesh, amplitudes, integrals, live_counts)


def solution(mesh):
    return jax.shard_map(
        functools.partial(on_device, mesh),
        mesh=mesh,
        in_specs=(P("pair", None, None), P("pair", "grp"), P()),
        out_specs=P("pair", None, "grp"),
        check_vma=False,
    )
```

time: 74.4 us -> 76.6 us (1.030)
  Pallas kernels: 72.5 us -> 74.7 us
    pallas_call x1, Pallas kernels: 72.5 us -> 74.7 us  [fused(): pl.pallas_call(functools.partial(kernel, sizes), out_shape=jax.ShapeDtype...]
where the time goes in v4:
time: 76.6 us; the launch traced here: 76.4 us
  Pallas kernels  74.7 us (98%)
  local copies, waits for them, and re-layouts  1.72 us (2%)
    pallas_call x1, Pallas kernels, fused(): pl.pallas_call(functools.partial(kernel, sizes), out_shape=jax.ShapeDtype...  74.7 us
    unnamed x1, local copies, waits for them, and re-layouts  1.72 us

profile of v4, /device:TPU:0, one launch (start us, length us, event | category | flops | bytes accessed | tf_op | source)
XLA Modules:
  0.0 76.4 jit_solution(5502995872530701851)
XLA Ops:
  0.0 74.7 %shard_map.37 = bf16[72,2304]{1,0:T(8,128)(2,1)} custom-call(s32[2]{0:T(128)} %live_ref.1, bf16[72,9216]{1,0:T(8,128)(2,1)} %bitcast.3, bf16[1152,2304]{1,0:T(8,128)(2,1)} %w_hbm.1), custom_call_target="tpu_custom_call" | custom-call | flops 3057647616 | bytes 5308416 | tf_op jit(solution)/shard_map/pallas_call | solution.py:375
  74.7 1.7 %copy.5 = bf16[3,24,2304]{2,1,0:T(8,128)(2,1)} copy(bf16[3,24,2304]{2,1,0:T(8,128)(2,1)} %bitcast.2) | data formatting | bytes 663552

commit v5 on v4

--- a/solution.py
+++ b/solution.py
@@ -158,20 +158,16 @@
         for copy in chain_copies(chunk, step, group, side):
             copy.start()
 
-    def chain_chunk(chunk):
-        @pl.loop(0, chips - 1)
-        def _(step):
-            chain_step(chunk, step)
-
+    lag = jnp.where(jnp.logical_or(z == 0, z == chips - 1), 0, 1)
     log_step = math.log(2.0) / 256.0
     occ_pairs = [(i, j) for i in range(occ_rows) for j in range(occ_rows)]
 
-    def mirror_copy(chunk, step):
+    def mirror_copy(step):
         other = lax.rem(me + step, devices)
         to_grp, to_pair = other // pairs, lax.rem(other, pairs)
         return pltpu.make_async_remote_copy(
-            src_ref=mirrored_ref.at[chunk, to_pair, to_grp], dst_ref=mirror_ref.at[chunk, me],
-            send_sem=m_send.at[chunk, step], recv_sem=m_recv.at[chunk, me],
+            src_ref=mirrored_ref.at[to_pair, to_grp], dst_ref=mirror_ref.at[me],
+            send_sem=m_send.at[step], recv_sem=m_recv.at[me],
             device_id=(to_grp, to_pair), device_id_type=MESH,
         )
 
@@ -216,31 +212,24 @@
                 level = jnp.floor(jnp.log(peak) * (1.0 / log_step)) + 2.0
                 whole = jnp.floor(block * (STEPS * jnp.exp(level * -log_step)) + 0.5)
                 whole = jnp.where(lane == 127, level, whole).astype(jnp.int32)
-                mirrored_ref[chunk, q, h] = whole.astype(jnp.int16)
-
+                mirrored_ref[q, h, 16 * chunk:16 * chunk + 16] = whole.astype(jnp.int16)
+
+    def take_all():
         @pl.loop(1, devices)
         def _(step):
-            mirror_copy(chunk, step).start()
-
-        mirror_ref[chunk, me] = mirrored_ref[chunk, p, g]
-
-    def take_all():
-        for chunk in range(chunks):
-            @pl.loop(1, devices)
-            def _(step):
-                other = lax.rem(me + step, devices)
-                pltpu.make_async_remote_copy(
-                    src_ref=mirror_ref.at[chunk, other], dst_ref=mirror_ref.at[chunk, other],
-                    send_sem=m_send.at[chunk, step], recv_sem=m_recv.at[chunk, other],
-                    device_id=(g, sibling), device_id_type=MESH,
-                ).wait_recv()
+            other = lax.rem(me + step, devices)
+            pltpu.make_async_remote_copy(
+                src_ref=mirror_ref.at[other], dst_ref=mirror_ref.at[other],
+                send_sem=m_send.at[step], recv_sem=m_recv.at[other],
+                device_id=(g, sibling), device_id_type=MESH,
+            ).wait_recv()
 
         @pl.loop(0, pairs)
         def _(q):
             blocks = []
             for h in range(grps):
                 for chunk in range(chunks):
-                    block = mirror_ref[chunk, h * pairs + q].astype(jnp.int32).astype(jnp.float32)
+                    block = mirror_ref[h * pairs + q, 16 * chunk:16 * chunk + 16].astype(jnp.int32).astype(jnp.float32)
                     blocks.append(block * (jnp.exp(block[:, 127:] * log_step) * (1.0 / STEPS)))
             rest = [jnp.zeros((128 - vb, 128), jnp.float32)]
             for end in range(2):
@@ -286,33 +275,28 @@
         tt_ref[...] = (both * mask_ref[:1, :]).astype(jnp.bfloat16)
 
         for chunk in range(chunks):
-            @pl.loop(0, width // 256)
-            def _(tile):
-                at = pl.ds(pl.multiple_of(chunk * width + tile * 256, 256), 256)
-                part_ref[chunk, group, :, pl.ds(pl.multiple_of(tile * 256, 256), 256)] = jnp.dot(
-                    tt_ref[...], w_ref[:, at], preferred_element_type=jnp.float32
-                )
-
+            part_ref[chunk, group] = jnp.dot(
+                tt_ref[...], w_ref[:, chunk * width:(chunk + 1) * width],
+                preferred_element_type=jnp.float32,
+            )
             cross_copy(chunk, group).start()
 
-        @pl.when(step < chips - 1)
-        def _():
-            chain_step(0, step)
-
-    at_end = jnp.logical_or(z == 0, z == chips - 1)
-
-    @pl.when(at_end)
-    def _():
-        for chunk in range(1, chunks):
-            chain_chunk(chunk)
+        turn = step - lag
+
+        @pl.when(jnp.logical_and(turn >= 0, turn < chips - 1))
+        def _():
+            @pl.loop(0, chunks)
+            def _(chunk):
+                chain_step(chunk, turn)
 
     for chunk in range(chunks):
-        if chunk > 0:
-            @pl.when(jnp.logical_not(at_end))
-            def _():
-                chain_chunk(chunk)
         finish_chunk(chunk)
 
+    @pl.loop(1, devices)
+    def _(step):
+        mirror_copy(step).start()
+
+    mirror_ref[me] = mirrored_ref[p, g]
     take_all()
 
     lane = lax.broadcasted_iota(jnp.int32, (rows, vb), 1)
@@ -357,8 +341,7 @@
 
     @pl.loop(1, devices)
     def _(step):
-        for chunk in range(chunks):
-            mirror_copy(chunk, step).wait_send()
+        mirror_copy(step).wait_send()
 
 
 def fused(mesh, amplitudes, integrals, live_counts):
@@ -396,13 +379,13 @@
             pltpu.VMEM((chunks, rows, width + 128), f32),
             pltpu.VMEM((rows * lanes, 128), f32),
             pltpu.VMEM((rows * 8, 128), f32),
-            pltpu.VMEM((chunks, pairs, grps, 16, 128), i16),
-            pltpu.VMEM((chunks, devices, 16, 128), i16),
+            pltpu.VMEM((pairs, grps, 16 * chunks, 128), i16),
+            pltpu.VMEM((devices, 16 * chunks, 128), i16),
             dma(()), dma((chips,)), dma((chips - 1, grps - 1)), dma((pairs,)),
             dma((chunks, chips)), dma((chunks, chips)),
             dma((chunks, chips - 1)), dma((chunks, chips - 1)),
             dma((chunks, 2, chips)), dma((chunks, 2, chips)),
-            dma((chunks, devices)), dma((chunks, devices)),
+            dma((devices,)), dma((devices,)),
         ],
         compiler_params=pltpu.CompilerParams(
             collective_id=0, has_side_effects=True, vmem_limit_bytes=VMEM_BYTES

time: 76.6 us -> 65.7 us (0.86)
  Pallas kernels: 74.7 us -> 63.8 us
    pallas_call x1, Pallas kernels: 74.7 us -> 63.8 us  [fused(): pl.pallas_call(functools.partial(kernel, sizes), out_shape=jax.ShapeDtype...]
where the time goes in v5:
time: 65.7 us; the launch traced here: 65.6 us
  Pallas kernels  63.8 us (97%)
  local copies, waits for them, and re-layouts  1.72 us (3%)
    pallas_call x1, Pallas kernels, fused(): pl.pallas_call(functools.partial(kernel, sizes), out_shape=jax.ShapeDtype...  63.8 us
    unnamed x1, local copies, waits for them, and re-layouts  1.72 us

profile of v5, /device:TPU:0, one launch (start us, length us, event | category | flops | bytes accessed | tf_op | source)
XLA Modules:
  0.0 65.6 jit_solution(383936705022026472)
XLA Ops:
  0.0 63.8 %shard_map.37 = bf16[72,2304]{1,0:T(8,128)(2,1)} custom-call(s32[2]{0:T(128)} %live_ref.1, bf16[72,9216]{1,0:T(8,128)(2,1)} %bitcast.3, bf16[1152,2304]{1,0:T(8,128)(2,1)} %w_hbm.1), custom_call_target="tpu_custom_call" | custom-call | flops 3057647616 | bytes 5308416 | tf_op jit(solution)/shard_map/pallas_call | solution.py:358
  63.8 1.7 %copy.5 = bf16[3,24,2304]{2,1,0:T(8,128)(2,1)} copy(bf16[3,24,2304]{2,1,0:T(8,128)(2,1)} %bitcast.2) | data formatting | bytes 663552

commit v6 on v5

--- a/solution.py
+++ b/solution.py
@@ -44,12 +44,11 @@
 
     barrier = pltpu.get_barrier_semaphore()
 
-    @pl.loop(1, devices)
-    def _(step):
-        other = lax.rem(me + step, devices)
-        pl.semaphore_signal(
-            barrier, inc=1, device_id=(other // pairs, lax.rem(other, pairs)), device_id_type=MESH
-        )
+    to_grps = [lax.rem(g + n, grps) for n in range(grps)]
+    to_pairs = [lax.rem(p + n, pairs) for n in range(pairs)]
+    others = [(to_grps[n], to_pairs[m]) for m in range(pairs) for n in range(grps)][1:]
+    for other in others:
+        pl.semaphore_signal(barrier, inc=1, device_id=other, device_id_type=MESH)
 
     w_copy = pltpu.make_async_copy(w_hbm, w_ref, w_sem)
     w_copy.start()
@@ -59,14 +58,29 @@
         mask_ref[:, c * vb:(c + 1) * vb] = jnp.where(lane < alive, 1.0, 0.0)
     pl.semaphore_wait(barrier, devices - 1)
 
-    def amp_cols(pair):
-        return amp_ref.at[:, pl.ds(pl.multiple_of(pair * depth, 128), depth)]
-
-    def t_copy(src, slot, send_sem, to_grp, to_pair):
+    pieces_t = t_ref.shape[1]
+    piece_cols = depth // pieces_t
+
+    def amp_cols(pair, piece):
+        return amp_ref.at[
+            :, pl.ds(pl.multiple_of(pair * depth + piece * piece_cols, 128), piece_cols)
+        ]
+
+    def t_copy(src, slot, piece, send_sem, to_grp, to_pair):
         return pltpu.make_async_remote_copy(
-            src_ref=src, dst_ref=t_ref.at[slot], send_sem=send_sem, recv_sem=t_recv.at[slot],
+            src_ref=src, dst_ref=t_ref.at[slot, piece], send_sem=send_sem,
+            recv_sem=t_recv.at[slot, piece],
             device_id=(to_grp, to_pair), device_id_type=MESH,
         )
+
+    def t_wait(slot, piece):
+        t_copy(t_ref.at[slot, piece], slot, piece, t_send.at[0], g, sibling).wait_recv()
+
+    def wait_sent(ref, send_sem):
+        pltpu.make_async_remote_copy(
+            src_ref=ref, dst_ref=ref, send_sem=send_sem, recv_sem=t_recv.at[0, 0],
+            device_id=(g, sibling), device_id_type=MESH,
+        ).wait_send()
 
     near_low = z < chips // 2
 
@@ -79,42 +93,38 @@
     sends_t = core == grp_src
     relays_t = core == grp_dst
 
-    def z_copy(step):
-        to = 2 * group_of(step) + grp_dst
-        return t_copy(amp_cols(to), p, t_send.at[step], g, to)
-
-    own_copy = pltpu.make_async_copy(amp_cols(p), t_ref.at[p], t_recv.at[p])
-    sib_copy = t_copy(amp_cols(sibling), p, t_send.at[chips - 1], g, sibling)
+    def own_copy(piece):
+        return pltpu.make_async_copy(amp_cols(p, piece), t_ref.at[p, piece], t_recv.at[p, piece])
 
     @pl.when(sends_t)
     def _():
         @pl.loop(0, chips - 1)
         def _(step):
-            z_copy(step).start()
-
-    own_copy.start()
-    sib_copy.start()
-
-    def relay_copy(step, hop):
-        slot = 2 * group_of(step) + grp_src
-        return t_copy(t_ref.at[slot], slot, t_fwd.at[step, hop - 1], lax.rem(g + hop, grps), p)
+            to = 2 * group_of(step) + grp_dst
+            for piece in range(pieces_t):
+                t_copy(amp_cols(to, piece), p, piece, t_send.at[0], g, to).start()
+
+    for piece in range(pieces_t):
+        own_copy(piece).start()
+        t_copy(amp_cols(sibling, piece), p, piece, t_send.at[1], g, sibling).start()
 
     def relay(step):
         @pl.when(relays_t)
         def _():
             slot = 2 * group_of(step) + grp_src
-            t_copy(t_ref.at[slot], slot, t_send.at[0], g, p).wait_recv()
-
-            @pl.loop(1, grps)
-            def _(hop):
-                relay_copy(step, hop).start()
+            for piece in range(pieces_t):
+                t_wait(slot, piece)
+                for hop in range(1, grps):
+                    t_copy(
+                        t_ref.at[slot, piece], slot, piece, t_fwd.at[hop - 1], to_grps[hop], p
+                    ).start()
 
     def cross_copy(chunk, group):
         return pltpu.make_async_remote_copy(
             src_ref=part_ref.at[
                 chunk, group, pl.ds(pl.multiple_of((1 - core) * rows, 8), rows)
             ],
-            dst_ref=cross_ref.at[chunk, group], send_sem=x_send.at[chunk, group],
+            dst_ref=cross_ref.at[chunk, group], send_sem=x_send,
             recv_sem=x_recv.at[chunk, group], device_id=(g, sibling), device_id_type=MESH,
         )
 
@@ -122,12 +132,12 @@
         to = 2 * (z + 1 - 2 * side) + core
         quanta = pltpu.make_async_remote_copy(
             src_ref=send_q.at[chunk, step], dst_ref=recv_q.at[chunk, side, group],
-            send_sem=q_send.at[chunk, step], recv_sem=q_recv.at[chunk, side, group],
+            send_sem=q_send, recv_sem=q_recv.at[chunk, side, group],
             device_id=(g, to), device_id_type=MESH,
         )
         scales = pltpu.make_async_remote_copy(
             src_ref=send_s.at[chunk, step], dst_ref=recv_s.at[chunk, side, group],
-            send_sem=s_send.at[chunk, step], recv_sem=s_recv.at[chunk, side, group],
+            send_sem=s_send, recv_sem=s_recv.at[chunk, side, group],
             device_id=(g, to), device_id_type=MESH,
         )
         return quanta, scales
@@ -162,13 +172,19 @@
     log_step = math.log(2.0) / 256.0
     occ_pairs = [(i, j) for i in range(occ_rows) for j in range(occ_rows)]
 
-    def mirror_copy(step):
-        other = lax.rem(me + step, devices)
-        to_grp, to_pair = other // pairs, lax.rem(other, pairs)
+    def mirror_copy(chunk, other):
+        to_grp, to_pair = other
         return pltpu.make_async_remote_copy(
-            src_ref=mirrored_ref.at[to_pair, to_grp], dst_ref=mirror_ref.at[me],
-            send_sem=m_send.at[step], recv_sem=m_recv.at[me],
+            src_ref=mirrored_ref.at[chunk, to_pair, to_grp], dst_ref=mirror_ref.at[chunk, me],
+            send_sem=m_send.at[chunk], recv_sem=m_recv.at[chunk],
             device_id=(to_grp, to_pair), device_id_type=MESH,
+        )
+
+    def mirror_all(chunk):
+        every = mirror_ref.at[chunk, pl.ds(0, devices - 1)]
+        return pltpu.make_async_remote_copy(
+            src_ref=every, dst_ref=every, send_sem=m_send.at[chunk], recv_sem=m_recv.at[chunk],
+            device_id=(g, sibling), device_id_type=MESH,
         )
 
     def finish_chunk(chunk):
@@ -212,24 +228,22 @@
                 level = jnp.floor(jnp.log(peak) * (1.0 / log_step)) + 2.0
                 whole = jnp.floor(block * (STEPS * jnp.exp(level * -log_step)) + 0.5)
                 whole = jnp.where(lane == 127, level, whole).astype(jnp.int32)
-                mirrored_ref[q, h, 16 * chunk:16 * chunk + 16] = whole.astype(jnp.int16)
+                mirrored_ref[chunk, q, h] = whole.astype(jnp.int16)
+
+        for other in others:
+            mirror_copy(chunk, other).start()
+        mirror_ref[chunk, me] = mirrored_ref[chunk, p, g]
 
     def take_all():
-        @pl.loop(1, devices)
-        def _(step):
-            other = lax.rem(me + step, devices)
-            pltpu.make_async_remote_copy(
-                src_ref=mirror_ref.at[other], dst_ref=mirror_ref.at[other],
-                send_sem=m_send.at[step], recv_sem=m_recv.at[other],
-                device_id=(g, sibling), device_id_type=MESH,
-            ).wait_recv()
+        for chunk in range(chunks):
+            mirror_all(chunk).wait_recv()
 
         @pl.loop(0, pairs)
         def _(q):
             blocks = []
             for h in range(grps):
                 for chunk in range(chunks):
-                    block = mirror_ref[h * pairs + q, 16 * chunk:16 * chunk + 16].astype(jnp.int32).astype(jnp.float32)
+                    block = mirror_ref[chunk, h * pairs + q].astype(jnp.int32).astype(jnp.float32)
                     blocks.append(block * (jnp.exp(block[:, 127:] * log_step) * (1.0 / STEPS)))
             rest = [jnp.zeros((128 - vb, 128), jnp.float32)]
             for end in range(2):
@@ -260,19 +274,23 @@
 
             @pl.when(jnp.logical_and(local, c == core))
             def _():
-                own_copy.wait()
+                for piece in range(pieces_t):
+                    own_copy(piece).wait()
 
             @pl.when(jnp.logical_or(
                 jnp.logical_and(local, c != core),
                 jnp.logical_and(jnp.logical_not(local), jnp.logical_not(relayed)),
             ))
             def _():
-                t_copy(t_ref.at[slot], slot, t_send.at[0], g, p).wait_recv()
-
-        both = jnp.concatenate(
-            [t_ref[2 * group].astype(jnp.float32), t_ref[2 * group + 1].astype(jnp.float32)], axis=0
-        )
-        tt_ref[...] = (both * mask_ref[:1, :]).astype(jnp.bfloat16)
+                for piece in range(pieces_t):
+                    t_wait(slot, piece)
+
+        for piece in range(pieces_t):
+            at = slice(piece * piece_cols, (piece + 1) * piece_cols)
+            both = jnp.concatenate(
+                [t_ref[2 * group + c, piece].astype(jnp.float32) for c in range(2)], axis=0
+            )
+            tt_ref[:, at] = (both * mask_ref[:1, at]).astype(jnp.bfloat16)
 
         for chunk in range(chunks):
             part_ref[chunk, group] = jnp.dot(
@@ -292,11 +310,6 @@
     for chunk in range(chunks):
         finish_chunk(chunk)
 
-    @pl.loop(1, devices)
-    def _(step):
-        mirror_copy(step).start()
-
-    mirror_ref[me] = mirrored_ref[p, g]
     take_all()
 
     lane = lax.broadcasted_iota(jnp.int32, (rows, vb), 1)
@@ -311,37 +324,22 @@
             total_ref[:, a * vb:(a + 1) * vb] = jnp.where(lane < alive, both, 0.0)
         out_ref[:, chunk * width:(chunk + 1) * width] = total_ref[...].astype(jnp.bfloat16)
 
-    sib_copy.wait_send()
-
     @pl.when(sends_t)
     def _():
-        @pl.loop(0, chips - 1)
-        def _(step):
-            z_copy(step).wait_send()
+        wait_sent(t_ref.at[pl.ds(0, chips - 1)], t_send.at[0])
+
+    wait_sent(t_ref.at[0], t_send.at[1])
 
     @pl.when(relays_t)
     def _():
-        @pl.loop(0, chips - 1)
-        def _(step):
-            @pl.loop(1, grps)
-            def _(hop):
-                relay_copy(step, hop).wait_send()
-
-    @pl.loop(0, chips)
-    def _(group):
-        for chunk in range(chunks):
-            cross_copy(chunk, group).wait_send()
-
-    @pl.loop(0, chips - 1)
-    def _(step):
-        group = group_of(step)
-        for chunk in range(chunks):
-            for copy in chain_copies(chunk, step, group, jnp.where(group > z, 0, 1)):
-                copy.wait_send()
-
-    @pl.loop(1, devices)
-    def _(step):
-        mirror_copy(step).wait_send()
+        for hop in range(1, grps):
+            wait_sent(t_ref.at[pl.ds(0, chips - 1)], t_fwd.at[hop - 1])
+
+    wait_sent(cross_ref, x_send)
+    wait_sent(send_q, q_send)
+    wait_sent(send_s, s_send)
+    for chunk in range(chunks):
+        mirror_all(chunk).wait_send()
 
 
 def fused(mesh, amplitudes, integrals, live_counts):
@@ -352,6 +350,7 @@
     lanes = cols // VB
     chunks = lanes // 8
     width = cols // chunks
+    pieces = 3 if depth % 384 == 0 else 1
     sizes = (grps, pairs, occ_rows, occupied, depth, cols, VB)
     f32, bf16, i16 = jnp.float32, jnp.bfloat16, jnp.int16
     dma = pltpu.SemaphoreType.DMA
@@ -366,7 +365,7 @@
         out_specs=pl.BlockSpec(memory_space=pltpu.VMEM),
         scratch_shapes=[
             pltpu.VMEM((depth, cols), bf16),
-            pltpu.VMEM((pairs, rows, depth), bf16),
+            pltpu.VMEM((pairs, pieces, rows, depth // pieces), bf16),
             pltpu.VMEM((2 * rows, depth), bf16),
             pltpu.VMEM((8, depth), f32),
             pltpu.VMEM((chunks, chips, 2 * rows, width), f32),
@@ -379,13 +378,11 @@
             pltpu.VMEM((chunks, rows, width + 128), f32),
             pltpu.VMEM((rows * lanes, 128), f32),
             pltpu.VMEM((rows * 8, 128), f32),
-            pltpu.VMEM((pairs, grps, 16 * chunks, 128), i16),
-            pltpu.VMEM((devices, 16 * chunks, 128), i16),
-            dma(()), dma((chips,)), dma((chips - 1, grps - 1)), dma((pairs,)),
-            dma((chunks, chips)), dma((chunks, chips)),
-            dma((chunks, chips - 1)), dma((chunks, chips - 1)),
-            dma((chunks, 2, chips)), dma((chunks, 2, chips)),
-            dma((devices,)), dma((devices,)),
+            pltpu.VMEM((chunks, pairs, grps, 16, 128), i16),
+            pltpu.VMEM((chunks, devices, 16, 128), i16),
+            dma(()), dma((2,)), dma((grps - 1,)), dma((pairs, pieces)),
+            dma(()), dma((chunks, chips)), dma(()), dma(()),
+            dma((chunks, 2, chips)), dma((chunks, 2, chips)), dma((chunks,)), dma((chunks,)),
         ],
         compiler_params=pltpu.CompilerParams(
             collective_id=0, has_side_effects=True, vmem_limit_bytes=VMEM_BYTES

time: 65.7 us -> 66.6 us (1.014)
  Pallas kernels: 63.8 us -> 64.7 us
    pallas_call x1, Pallas kernels: 63.8 us -> 64.7 us  [fused(): pl.pallas_call(functools.partial(kernel, sizes), out_shape=jax.ShapeDtype...]
where the time goes in v6:
time: 66.6 us; the launch traced here: 66.4 us
  Pallas kernels  64.7 us (97%)
  local copies, waits for them, and re-layouts  1.72 us (3%)
    pallas_call x1, Pallas kernels, fused(): pl.pallas_call(functools.partial(kernel, sizes), out_shape=jax.ShapeDtype...  64.7 us
    unnamed x1, local copies, waits for them, and re-layouts  1.72 us

profile of v6, /device:TPU:0, one launch (start us, length us, event | category | flops | bytes accessed | tf_op | source)
XLA Modules:
  0.0 66.4 jit_solution(15059818061873077826)
XLA Ops:
  0.0 64.7 %shard_map.37 = bf16[72,2304]{1,0:T(8,128)(2,1)} custom-call(s32[2]{0:T(128)} %live_ref.1, bf16[72,9216]{1,0:T(8,128)(2,1)} %bitcast.3, bf16[1152,2304]{1,0:T(8,128)(2,1)} %w_hbm.1), custom_call_target="tpu_custom_call" | custom-call | flops 3057647616 | bytes 5308416 | tf_op jit(solution)/shard_map/pallas_call | solution.py:357
  64.7 1.7 %copy.5 = bf16[3,24,2304]{2,1,0:T(8,128)(2,1)} copy(bf16[3,24,2304]{2,1,0:T(8,128)(2,1)} %bitcast.2) | data formatting | bytes 663552

commit v7 on v6

--- a/solution.py
+++ b/solution.py
@@ -172,18 +172,18 @@
     log_step = math.log(2.0) / 256.0
     occ_pairs = [(i, j) for i in range(occ_rows) for j in range(occ_rows)]
 
-    def mirror_copy(chunk, other):
+    def mirror_copy(other):
         to_grp, to_pair = other
         return pltpu.make_async_remote_copy(
-            src_ref=mirrored_ref.at[chunk, to_pair, to_grp], dst_ref=mirror_ref.at[chunk, me],
-            send_sem=m_send.at[chunk], recv_sem=m_recv.at[chunk],
+            src_ref=mirrored_ref.at[to_pair, to_grp], dst_ref=mirror_ref.at[me],
+            send_sem=m_send, recv_sem=m_recv,
             device_id=(to_grp, to_pair), device_id_type=MESH,
         )
 
-    def mirror_all(chunk):
-        every = mirror_ref.at[chunk, pl.ds(0, devices - 1)]
+    def mirror_all():
+        every = mirror_ref.at[pl.ds(0, devices - 1)]
         return pltpu.make_async_remote_copy(
-            src_ref=every, dst_ref=every, send_sem=m_send.at[chunk], recv_sem=m_recv.at[chunk],
+            src_ref=every, dst_ref=every, send_sem=m_send, recv_sem=m_recv,
             device_id=(g, sibling), device_id_type=MESH,
         )
 
@@ -202,7 +202,7 @@
         for a in range(8):
             piece_ref[pl.ds(a, rows, stride=8), :] = final_ref[chunk, :, a * vb:a * vb + 128]
 
-        @pl.loop(0, pairs)
+        @pl.loop(0, pairs, unroll=4)
         def _(q):
             lane = lax.broadcasted_iota(jnp.int32, (16, 128), 1)
             pieces = [
@@ -228,22 +228,17 @@
                 level = jnp.floor(jnp.log(peak) * (1.0 / log_step)) + 2.0
                 whole = jnp.floor(block * (STEPS * jnp.exp(level * -log_step)) + 0.5)
                 whole = jnp.where(lane == 127, level, whole).astype(jnp.int32)
-                mirrored_ref[chunk, q, h] = whole.astype(jnp.int16)
-
-        for other in others:
-            mirror_copy(chunk, other).start()
-        mirror_ref[chunk, me] = mirrored_ref[chunk, p, g]
+                mirrored_ref[q, h, 16 * chunk:16 * chunk + 16] = whole.astype(jnp.int16)
 
     def take_all():
-        for chunk in range(chunks):
-            mirror_all(chunk).wait_recv()
-
-        @pl.loop(0, pairs)
+        mirror_all().wait_recv()
+
+        @pl.loop(0, pairs, unroll=4)
         def _(q):
             blocks = []
             for h in range(grps):
                 for chunk in range(chunks):
-                    block = mirror_ref[chunk, h * pairs + q].astype(jnp.int32).astype(jnp.float32)
+                    block = mirror_ref[h * pairs + q, 16 * chunk:16 * chunk + 16].astype(jnp.int32).astype(jnp.float32)
                     blocks.append(block * (jnp.exp(block[:, 127:] * log_step) * (1.0 / STEPS)))
             rest = [jnp.zeros((128 - vb, 128), jnp.float32)]
             for end in range(2):
@@ -285,6 +280,8 @@
                 for piece in range(pieces_t):
                     t_wait(slot, piece)
 
+        turn = step - lag
+        turning = jnp.logical_and(turn >= 0, turn < chips - 1)
         for piece in range(pieces_t):
             at = slice(piece * piece_cols, (piece + 1) * piece_cols)
             both = jnp.concatenate(
@@ -298,18 +295,21 @@
                 preferred_element_type=jnp.float32,
             )
             cross_copy(chunk, group).start()
-
-        turn = step - lag
-
-        @pl.when(jnp.logical_and(turn >= 0, turn < chips - 1))
-        def _():
-            @pl.loop(0, chunks)
-            def _(chunk):
-                chain_step(chunk, turn)
+            if chunk > 0:
+                @pl.when(turning)
+                def _():
+                    chain_step(chunk - 1, turn)
+
+        @pl.when(turning)
+        def _():
+            chain_step(chunks - 1, turn)
 
     for chunk in range(chunks):
         finish_chunk(chunk)
 
+    for other in others:
+        mirror_copy(other).start()
+    mirror_ref[me] = mirrored_ref[p, g]
     take_all()
 
     lane = lax.broadcasted_iota(jnp.int32, (rows, vb), 1)
@@ -338,8 +338,7 @@
     wait_sent(cross_ref, x_send)
     wait_sent(send_q, q_send)
     wait_sent(send_s, s_send)
-    for chunk in range(chunks):
-        mirror_all(chunk).wait_send()
+    mirror_all().wait_send()
 
 
 def fused(mesh, amplitudes, integrals, live_counts):
@@ -378,11 +377,11 @@
             pltpu.VMEM((chunks, rows, width + 128), f32),
             pltpu.VMEM((rows * lanes, 128), f32),
             pltpu.VMEM((rows * 8, 128), f32),
-            pltpu.VMEM((chunks, pairs, grps, 16, 128), i16),
-            pltpu.VMEM((chunks, devices, 16, 128), i16),
+            pltpu.VMEM((pairs, grps, 16 * chunks, 128), i16),
+            pltpu.VMEM((devices, 16 * chunks, 128), i16),
             dma(()), dma((2,)), dma((grps - 1,)), dma((pairs, pieces)),
             dma(()), dma((chunks, chips)), dma(()), dma(()),
-            dma((chunks, 2, chips)), dma((chunks, 2, chips)), dma((chunks,)), dma((chunks,)),
+            dma((chunks, 2, chips)), dma((chunks, 2, chips)), dma(()), dma(()),
         ],
         compiler_params=pltpu.CompilerParams(
             collective_id=0, has_side_effects=True, vmem_limit_bytes=VMEM_BYTES

time: 66.6 us -> 62.8 us (0.943)
  the two profiles are of different devices: /device:TPU:0 before, /device:TPU:17 now
where the time goes in v7:
time: 62.8 us; the launch traced here: 62.6 us
  Pallas kernels  60.9 us (97%)
  local copies, waits for them, and re-layouts  1.72 us (3%)
    pallas_call x1, Pallas kernels, fused(): pl.pallas_call(functools.partial(kernel, sizes), out_shape=jax.ShapeDtype...  60.9 us
    unnamed x1, local copies, waits for them, and re-layouts  1.72 us

profile of v7, /device:TPU:17, one launch (start us, length us, event | category | flops | bytes accessed | tf_op | source)
XLA Modules:
  0.0 62.6 jit_solution(1722584851276492430)
XLA Ops:
  0.0 60.9 %shard_map.37 = bf16[72,2304]{1,0:T(8,128)(2,1)} custom-call(s32[2]{0:T(128)} %live_ref.1, bf16[72,9216]{1,0:T(8,128)(2,1)} %bitcast.3, bf16[1152,2304]{1,0:T(8,128)(2,1)} %w_hbm.1), custom_call_target="tpu_custom_call" | custom-call | flops 3057647616 | bytes 5308416 | tf_op jit(solution)/shard_map/pallas_call | solution.py:356
  60.9 1.7 %copy.5 = bf16[3,24,2304]{2,1,0:T(8,128)(2,1)} copy(bf16[3,24,2304]{2,1,0:T(8,128)(2,1)} %bitcast.2) | data formatting | bytes 663552

commit v8 on v7

--- a/solution.py
+++ b/solution.py
@@ -11,7 +11,7 @@
 VB = 96
 STEPS = 32767.0
 MESH = pl.DeviceIdType.MESH
-VMEM_BYTES = 58 * 2**20
+VMEM_BYTES = 40 * 2**20
 
 
 def quantize(value):
@@ -249,39 +249,7 @@
                         turned[at * lanes:(at + 1) * lanes]
                     )
 
-    relay(0)
-    w_copy.wait()
-    for chunk in range(chunks):
-        final_ref[chunk, :, width:] = jnp.zeros((rows, 128), jnp.float32)
-
-    @pl.loop(0, chips)
-    def _(step):
-        group = group_of(step)
-
-        @pl.when(step < chips - 2)
-        def _():
-            relay(step + 1)
-
-        for c in range(2):
-            slot = 2 * group + c
-            local = step == chips - 1
-            relayed = jnp.logical_and(relays_t, c == grp_src)
-
-            @pl.when(jnp.logical_and(local, c == core))
-            def _():
-                for piece in range(pieces_t):
-                    own_copy(piece).wait()
-
-            @pl.when(jnp.logical_or(
-                jnp.logical_and(local, c != core),
-                jnp.logical_and(jnp.logical_not(local), jnp.logical_not(relayed)),
-            ))
-            def _():
-                for piece in range(pieces_t):
-                    t_wait(slot, piece)
-
-        turn = step - lag
-        turning = jnp.logical_and(turn >= 0, turn < chips - 1)
+    def mask_group(group):
         for piece in range(pieces_t):
             at = slice(piece * piece_cols, (piece + 1) * piece_cols)
             both = jnp.concatenate(
@@ -289,20 +257,57 @@
             )
             tt_ref[:, at] = (both * mask_ref[:1, at]).astype(jnp.bfloat16)
 
+    def multiply(chunk, group):
+        part_ref[chunk, group] = jnp.dot(
+            tt_ref[...], w_ref[:, chunk * width:(chunk + 1) * width],
+            preferred_element_type=jnp.float32,
+        )
+        cross_copy(chunk, group).start()
+
+    for chunk in range(chunks):
+        final_ref[chunk, :, width:] = jnp.zeros((rows, 128), jnp.float32)
+    w_copy.wait()
+    for piece in range(pieces_t):
+        own_copy(piece).wait()
+        t_wait(sibling, piece)
+    mask_group(z)
+    multiply(0, z)
+    relay(0)
+    for chunk in range(1, chunks):
+        multiply(chunk, z)
+
+    @pl.loop(0, chips - 1)
+    def _(step):
+        group = group_of(step)
+
+        @pl.when(step < chips - 2)
+        def _():
+            relay(step + 1)
+
+        for c in range(2):
+            @pl.when(jnp.logical_not(jnp.logical_and(relays_t, c == grp_src)))
+            def _():
+                for piece in range(pieces_t):
+                    t_wait(2 * group + c, piece)
+
+        turn = step - lag
+        mask_group(group)
         for chunk in range(chunks):
-            part_ref[chunk, group] = jnp.dot(
-                tt_ref[...], w_ref[:, chunk * width:(chunk + 1) * width],
-                preferred_element_type=jnp.float32,
-            )
-            cross_copy(chunk, group).start()
+            multiply(chunk, group)
             if chunk > 0:
-                @pl.when(turning)
+                @pl.when(turn >= 0)
                 def _():
                     chain_step(chunk - 1, turn)
 
-        @pl.when(turning)
+        @pl.when(turn >= 0)
         def _():
             chain_step(chunks - 1, turn)
+
+    @pl.when(lag == 1)
+    def _():
+        @pl.loop(0, chunks)
+        def _(chunk):
+            chain_step(chunk, chips - 2)
 
     for chunk in range(chunks):
         finish_chunk(chunk)
@@ -358,8 +363,8 @@
         out_shape=jax.ShapeDtypeStruct((rows, cols), bf16),
         in_specs=[
             pl.BlockSpec(memory_space=pltpu.SMEM),
-            pl.BlockSpec(memory_space=pl.ANY),
-            pl.BlockSpec(memory_space=pl.ANY),
+            pl.BlockSpec(memory_space=pltpu.HBM),
+            pl.BlockSpec(memory_space=pltpu.HBM),
         ],
         out_specs=pl.BlockSpec(memory_space=pltpu.VMEM),
         scratch_shapes=[

time: 62.8 us -> 64.7 us (1.030)
  the two profiles are of different devices: /device:TPU:17 before, /device:TPU:9 now
where the time goes in v8:
time: 64.7 us; the launch traced here: 64.5 us
  Pallas kernels  59.3 us (92%)
  local copies, waits for them, and re-layouts  5.21 us (8%)
    pallas_call x1, Pallas kernels, fused(): pl.pallas_call(functools.partial(kernel, sizes), out_shape=jax.ShapeDtype...  59.3 us
    unnamed x7, local copies, waits for them, and re-layouts  5.21 us

profile of v8, /device:TPU:9, one launch (start us, length us, event | category | flops | bytes accessed | tf_op | source)
XLA Modules:
  0.0 64.5 jit_solution(3914409161581216646)
XLA Ops:
  0.0 0.0 copy-start
  0.0 2.5 %copy-done = bf16[1152,2304]{1,0:T(8,128)(2,1)S(1)} copy-done((bf16[1152,2304]{1,0:T(8,128)(2,1)S(1)}, bf16[1152,2304]{1,0:T(8,128)(2,1)}, u32[]{:S(2)}) %copy-start) | copy-done | bytes 5308440
  2.5 0.0 copy-start.1
  2.5 1.3 %copy-done.1 = bf16[3,24,9216]{2,1,0:T(8,128)(2,1)S(1)} copy-done((bf16[3,24,9216]{2,1,0:T(8,128)(2,1)S(1)}, bf16[3,24,9216]{2,1,0:T(8,128)(2,1)}, u32[]{:S(2)}) %copy-start.1) | copy-done | bytes 1327128
  3.8 0.0 copy-start.2
  3.8 0.7 %copy-done.2 = s32[2]{0:T(128)S(1)} copy-done((s32[2]{0:T(128)S(1)}, s32[2]{0:T(128)}, u32[]{:S(2)}) %copy-start.2) | copy-done | bytes 32
  4.5 59.3 %shard_map.37 = bf16[72,2304]{1,0:T(8,128)(2,1)S(1)} custom-call(s32[2]{0:T(128)S(1)} %copy-done.2, bf16[72,9216]{1,0:T(8,128)(2,1)S(1)} %bitcast.3, bf16[1152,2304]{1,0:T(8,128)(2,1)S(1)} %copy-done), custom_call_target="tpu_custom_call" | custom-call | flops 3057647616 | bytes 5308416 | tf_op jit(solution)/shard_map/pallas_call | solution.py:361
  63.7 0.7 %copy.5 = bf16[3,24,2304]{2,1,0:T(8,128)(2,1)} copy(bf16[3,24,2304]{2,1,0:T(8,128)(2,1)S(1)} %bitcast.2) | data formatting | bytes 663552
Async XLA Ops:
  0.0 2.5 %copy-start = (bf16[1152,2304]{1,0:T(8,128)(2,1)S(1)}, bf16[1152,2304]{1,0:T(8,128)(2,1)}, u32[]{:S(2)}) copy-start(bf16[1152,2304]{1,0:T(8,128)(2,1)} %w_hbm.1) | copy-start | bytes 15925252
  2.5 1.3 %copy-start.1 = (bf16[3,24,9216]{2,1,0:T(8,128)(2,1)S(1)}, bf16[3,24,9216]{2,1,0:T(8,128)(2,1)}, u32[]{:S(2)}) copy-start(bf16[3,24,9216]{2,1,0:T(8,128)(2,1)} %param.3) | copy-start | bytes 3981316
  3.8 0.7 %copy-start.2 = (s32[2]{0:T(128)S(1)}, s32[2]{0:T(128)}, u32[]{:S(2)}) copy-start(s32[2]{0:T(128)} %live_ref.1) | copy-start | bytes 28

commit v9 on v8

--- a/solution.py
+++ b/solution.py
@@ -11,7 +11,7 @@
 VB = 96
 STEPS = 32767.0
 MESH = pl.DeviceIdType.MESH
-VMEM_BYTES = 40 * 2**20
+VMEM_BYTES = 58 * 2**20
 
 
 def quantize(value):
@@ -176,14 +176,14 @@
         to_grp, to_pair = other
         return pltpu.make_async_remote_copy(
             src_ref=mirrored_ref.at[to_pair, to_grp], dst_ref=mirror_ref.at[me],
-            send_sem=m_send, recv_sem=m_recv,
+            send_sem=m_send, recv_sem=m_recv.at[p],
             device_id=(to_grp, to_pair), device_id_type=MESH,
         )
 
-    def mirror_all():
-        every = mirror_ref.at[pl.ds(0, devices - 1)]
+    def mirror_part(count, recv_sem):
+        part = mirror_ref.at[pl.ds(0, count)]
         return pltpu.make_async_remote_copy(
-            src_ref=every, dst_ref=every, send_sem=m_send, recv_sem=m_recv,
+            src_ref=part, dst_ref=part, send_sem=m_send, recv_sem=recv_sem,
             device_id=(g, sibling), device_id_type=MESH,
         )
 
@@ -230,24 +230,21 @@
                 whole = jnp.where(lane == 127, level, whole).astype(jnp.int32)
                 mirrored_ref[q, h, 16 * chunk:16 * chunk + 16] = whole.astype(jnp.int16)
 
-    def take_all():
-        mirror_all().wait_recv()
-
-        @pl.loop(0, pairs, unroll=4)
-        def _(q):
-            blocks = []
-            for h in range(grps):
-                for chunk in range(chunks):
-                    block = mirror_ref[h * pairs + q, 16 * chunk:16 * chunk + 16].astype(jnp.int32).astype(jnp.float32)
-                    blocks.append(block * (jnp.exp(block[:, 127:] * log_step) * (1.0 / STEPS)))
-            rest = [jnp.zeros((128 - vb, 128), jnp.float32)]
-            for end in range(2):
-                turned = jnp.concatenate([b[8 * end:8 * end + 8] for b in blocks] + rest, axis=0).T
-                for at, (i, j) in enumerate(occ_pairs[end * slots:(end + 1) * slots]):
-                    row = (j * occupied + q * occ_rows + i) * lanes
-                    split_ref[pl.ds(pl.multiple_of(row, 8), lanes), :] = (
-                        turned[at * lanes:(at + 1) * lanes]
-                    )
+    def take_from(q, count):
+        mirror_part(count, m_recv.at[q]).wait_recv()
+        blocks = []
+        for h in range(grps):
+            for chunk in range(chunks):
+                block = mirror_ref[h * pairs + q, 16 * chunk:16 * chunk + 16].astype(jnp.int32).astype(jnp.float32)
+                blocks.append(block * (jnp.exp(block[:, 127:] * log_step) * (1.0 / STEPS)))
+        rest = [jnp.zeros((128 - vb, 128), jnp.float32)]
+        for end in range(2):
+            turned = jnp.concatenate([b[8 * end:8 * end + 8] for b in blocks] + rest, axis=0).T
+            for at, (i, j) in enumerate(occ_pairs[end * slots:(end + 1) * slots]):
+                row = (j * occupied + q * occ_rows + i) * lanes
+                split_ref[pl.ds(pl.multiple_of(row, 8), lanes), :] = (
+                    turned[at * lanes:(at + 1) * lanes]
+                )
 
     def mask_group(group):
         for piece in range(pieces_t):
@@ -315,7 +312,11 @@
     for other in others:
         mirror_copy(other).start()
     mirror_ref[me] = mirrored_ref[p, g]
-    take_all()
+    take_from(p, grps - 1)
+
+    @pl.loop(1, pairs)
+    def _(step):
+        take_from(lax.rem(p + pairs - step, pairs), grps)
 
     lane = lax.broadcasted_iota(jnp.int32, (rows, vb), 1)
     for chunk in range(chunks):
@@ -343,7 +344,7 @@
     wait_sent(cross_ref, x_send)
     wait_sent(send_q, q_send)
     wait_sent(send_s, s_send)
-    mirror_all().wait_send()
+    mirror_part(devices - 1, m_recv.at[0]).wait_send()
 
 
 def fused(mesh, amplitudes, integrals, live_counts):
@@ -386,7 +387,7 @@
             pltpu.VMEM((devices, 16 * chunks, 128), i16),
             dma(()), dma((2,)), dma((grps - 1,)), dma((pairs, pieces)),
             dma(()), dma((chunks, chips)), dma(()), dma(()),
-            dma((chunks, 2, chips)), dma((chunks, 2, chips)), dma(()), dma(()),
+            dma((chunks, 2, chips)), dma((chunks, 2, chips)), dma(()), dma((pairs,)),
         ],
         compiler_params=pltpu.CompilerParams(
             collective_id=0, has_side_effects=True, vmem_limit_bytes=VMEM_BYTES

time: 64.7 us -> 61.8 us (0.955)
  the two profiles are of different devices: /device:TPU:9 before, /device:TPU:0 now
where the time goes in v9:
time: 61.8 us; the launch traced here: 60.7 us
  Pallas kernels  59 us (95%)
  local copies, waits for them, and re-layouts  1.72 us (3%)
    pallas_call x1, Pallas kernels, fused(): pl.pallas_call(functools.partial(kernel, sizes), out_shape=jax.ShapeDtype...  59 us
    unnamed x1, local copies, waits for them, and re-layouts  1.72 us

profile of v9, /device:TPU:0, one launch (start us, length us, event | category | flops | bytes accessed | tf_op | source)
XLA Modules:
  0.0 60.7 jit_solution(17250316509383298905)
XLA Ops:
  0.0 59.0 %shard_map.37 = bf16[72,2304]{1,0:T(8,128)(2,1)} custom-call(s32[2]{0:T(128)} %live_ref.1, bf16[72,9216]{1,0:T(8,128)(2,1)} %bitcast.3, bf16[1152,2304]{1,0:T(8,128)(2,1)} %w_hbm.1), custom_call_target="tpu_custom_call" | custom-call | flops 3057647616 | bytes 5308416 | tf_op jit(solution)/shard_map/pallas_call | solution.py:362
  59.0 1.7 %copy.5 = bf16[3,24,2304]{2,1,0:T(8,128)(2,1)} copy(bf16[3,24,2304]{2,1,0:T(8,128)(2,1)} %bitcast.2) | data formatting | bytes 663552

commit v10 on v9

--- a/solution.py
+++ b/solution.py
@@ -46,7 +46,8 @@
 
     to_grps = [lax.rem(g + n, grps) for n in range(grps)]
     to_pairs = [lax.rem(p + n, pairs) for n in range(pairs)]
-    others = [(to_grps[n], to_pairs[m]) for m in range(pairs) for n in range(grps)][1:]
+    far_first = sorted(range(pairs), key=lambda m: (abs(m - pairs // 2), m))
+    others = [(to_grps[n], to_pairs[m]) for m in far_first for n in range(grps) if n or m]
     for other in others:
         pl.semaphore_signal(barrier, inc=1, device_id=other, device_id_type=MESH)
 
@@ -235,7 +236,8 @@
         blocks = []
         for h in range(grps):
             for chunk in range(chunks):
-                block = mirror_ref[h * pairs + q, 16 * chunk:16 * chunk + 16].astype(jnp.int32).astype(jnp.float32)
+                block = mirror_ref[h * pairs + q, 16 * chunk:16 * chunk + 16]
+                block = block.astype(jnp.int32).astype(jnp.float32)
                 blocks.append(block * (jnp.exp(block[:, 127:] * log_step) * (1.0 / STEPS)))
         rest = [jnp.zeros((128 - vb, 128), jnp.float32)]
         for end in range(2):
@@ -263,14 +265,13 @@
 
     for chunk in range(chunks):
         final_ref[chunk, :, width:] = jnp.zeros((rows, 128), jnp.float32)
+    relay(0)
     w_copy.wait()
     for piece in range(pieces_t):
         own_copy(piece).wait()
         t_wait(sibling, piece)
     mask_group(z)
-    multiply(0, z)
-    relay(0)
-    for chunk in range(1, chunks):
+    for chunk in range(chunks):
         multiply(chunk, z)
 
     @pl.loop(0, chips - 1)
@@ -312,11 +313,8 @@
     for other in others:
         mirror_copy(other).start()
     mirror_ref[me] = mirrored_ref[p, g]
-    take_from(p, grps - 1)
-
-    @pl.loop(1, pairs)
-    def _(step):
-        take_from(lax.rem(p + pairs - step, pairs), grps)
+    for m in far_first:
+        take_from(lax.rem(p + pairs - m, pairs), grps if m else grps - 1)
 
     lane = lax.broadcasted_iota(jnp.int32, (rows, vb), 1)
     for chunk in range(chunks):

time: 61.8 us -> 63.9 us (1.034); the launches traced: 60.7 us -> 63.7 us
  Pallas kernels: 59 us -> 62 us
    pallas_call x1, Pallas kernels: 59 us -> 62 us  [fused(): pl.pallas_call(functools.partial(kernel, sizes), out_shape=jax.ShapeDtype...]
where the time goes in v10:
time: 63.9 us; the launch traced here: 63.7 us
  Pallas kernels  62 us (97%)
  local copies, waits for them, and re-layouts  1.72 us (3%)
    pallas_call x1, Pallas kernels, fused(): pl.pallas_call(functools.partial(kernel, sizes), out_shape=jax.ShapeDtype...  62 us
    unnamed x1, local copies, waits for them, and re-layouts  1.72 us

profile of v10, /device:TPU:0, one launch (start us, length us, event | category | flops | bytes accessed | tf_op | source)
XLA Modules:
  0.0 63.7 jit_solution(13255069307565529792)
XLA Ops:
  0.0 62.0 %shard_map.37 = bf16[72,2304]{1,0:T(8,128)(2,1)} custom-call(s32[2]{0:T(128)} %live_ref.1, bf16[72,9216]{1,0:T(8,128)(2,1)} %bitcast.3, bf16[1152,2304]{1,0:T(8,128)(2,1)} %w_hbm.1), custom_call_target="tpu_custom_call" | custom-call | flops 3057647616 | bytes 5308416 | tf_op jit(solution)/shard_map/pallas_call | solution.py:360
  62.0 1.7 %copy.5 = bf16[3,24,2304]{2,1,0:T(8,128)(2,1)} copy(bf16[3,24,2304]{2,1,0:T(8,128)(2,1)} %bitcast.2) | data formatting | bytes 663552

commit v11 on v9

--- a/solution.py
+++ b/solution.py
@@ -42,6 +42,8 @@
     sibling = 2 * z + 1 - core
     me = g * pairs + p
 
+    w_copy = pltpu.make_async_copy(w_hbm, w_ref, w_sem)
+    w_copy.start()
     barrier = pltpu.get_barrier_semaphore()
 
     to_grps = [lax.rem(g + n, grps) for n in range(grps)]
@@ -50,12 +52,12 @@
     for other in others:
         pl.semaphore_signal(barrier, inc=1, device_id=other, device_id_type=MESH)
 
-    w_copy = pltpu.make_async_copy(w_hbm, w_ref, w_sem)
-    w_copy.start()
     for c in range(depth // vb):
         alive = jnp.where(p * (depth // vb) + c < live_ref[1], live_ref[1], 0)
         lane = lax.broadcasted_iota(jnp.int32, (8, vb), 1)
         mask_ref[:, c * vb:(c + 1) * vb] = jnp.where(lane < alive, 1.0, 0.0)
+    for chunk in range(chunks):
+        final_ref[chunk, :, width:] = jnp.zeros((rows, 128), jnp.float32)
     pl.semaphore_wait(barrier, devices - 1)
 
     pieces_t = t_ref.shape[1]
@@ -261,8 +263,6 @@
         )
         cross_copy(chunk, group).start()
 
-    for chunk in range(chunks):
-        final_ref[chunk, :, width:] = jnp.zeros((rows, 128), jnp.float32)
     w_copy.wait()
     for piece in range(pieces_t):
         own_copy(piece).wait()

time: 61.8 us -> 61.8 us (level)
  no operation moved by 1% of the time
where the time goes in v11:
time: 61.8 us; the launch traced here: 60.7 us
  Pallas kernels  59 us (95%)
  local copies, waits for them, and re-layouts  1.72 us (3%)
    pallas_call x1, Pallas kernels, fused(): pl.pallas_call(functools.partial(kernel, sizes), out_shape=jax.ShapeDtype...  59 us
    unnamed x1, local copies, waits for them, and re-layouts  1.72 us

profile of v11, /device:TPU:0, one launch (start us, length us, event | category | flops | bytes accessed | tf_op | source)
XLA Modules:
  0.0 60.7 jit_solution(16658384497471469427)
XLA Ops:
  0.0 59.0 %shard_map.37 = bf16[72,2304]{1,0:T(8,128)(2,1)} custom-call(s32[2]{0:T(128)} %live_ref.1, bf16[72,9216]{1,0:T(8,128)(2,1)} %bitcast.3, bf16[1152,2304]{1,0:T(8,128)(2,1)} %w_hbm.1), custom_call_target="tpu_custom_call" | custom-call | flops 3057647616 | bytes 5308416 | tf_op jit(solution)/shard_map/pallas_call | solution.py:362
  59.0 1.7 %copy.5 = bf16[3,24,2304]{2,1,0:T(8,128)(2,1)} copy(bf16[3,24,2304]{2,1,0:T(8,128)(2,1)} %bitcast.2) | data formatting | bytes 663552

commit v12 on v11

--- a/solution.py
+++ b/solution.py
@@ -355,7 +355,7 @@
     lanes = cols // VB
     chunks = lanes // 8
     width = cols // chunks
-    pieces = 3 if depth % 384 == 0 else 1
+    pieces = 1
     sizes = (grps, pairs, occ_rows, occupied, depth, cols, VB)
     f32, bf16, i16 = jnp.float32, jnp.bfloat16, jnp.int16
     dma = pltpu.SemaphoreType.DMA

time: 61.8 us -> 62.8 us (1.016)
  Pallas kernels: 59 us -> 60.1 us
    pallas_call x1, Pallas kernels: 59 us -> 60.1 us  [fused(): pl.pallas_call(functools.partial(kernel, sizes), out_shape=jax.ShapeDtype...]
where the time goes in v12:
time: 62.8 us; the launch traced here: 61.8 us
  Pallas kernels  60.1 us (96%)
  local copies, waits for them, and re-layouts  1.72 us (3%)
    pallas_call x1, Pallas kernels, fused(): pl.pallas_call(functools.partial(kernel, sizes), out_shape=jax.ShapeDtype...  60.1 us
    unnamed x1, local copies, waits for them, and re-layouts  1.72 us

profile of v12, /device:TPU:0, one launch (start us, length us, event | category | flops | bytes accessed | tf_op | source)
XLA Modules:
  0.0 61.8 jit_solution(14589657012145380043)
XLA Ops:
  0.0 60.1 %shard_map.37 = bf16[72,2304]{1,0:T(8,128)(2,1)} custom-call(s32[2]{0:T(128)} %live_ref.1, bf16[72,9216]{1,0:T(8,128)(2,1)} %bitcast.3, bf16[1152,2304]{1,0:T(8,128)(2,1)} %w_hbm.1), custom_call_target="tpu_custom_call" | custom-call | flops 3057647616 | bytes 5308416 | tf_op jit(solution)/shard_map/pallas_call | solution.py:362
  60.1 1.7 %copy.5 = bf16[3,24,2304]{2,1,0:T(8,128)(2,1)} copy(bf16[3,24,2304]{2,1,0:T(8,128)(2,1)} %bitcast.2) | data formatting | bytes 663552
